TPU v7x, 128 devices: a whole 4x4x4 slice. The times are simulated.
128 devices in a mesh: dp: 16 (over y, x_hi, core), tensor: 8 (over z, x_lo).
Axes of the slice: x: 4 (x_hi: 2, x_lo: 2; x = x_hi * 2 + x_lo), y: 4, z: 4, core: 2. Of those that a mesh axis runs over, the one named last changes fastest.
Arguments:
- hidden_in: bfloat16 [16, 1024, 2048], P('dp', 'tensor'), may hold values from -6 to 6
- segment_ids: int32 [16, 1024], P('dp'), may hold values from 0 to 2, as said below
- attention_gain: bfloat16 [2048], replicated, may hold values from 0.5 to 2
- mlp_gain: bfloat16 [2048], replicated, may hold values from 0.5 to 2
- query_base: bfloat16 [2048, 2048], P(None, 'tensor'), may hold values from -0.125 to 0.125
- query_left: float32 [2048, 16], replicated, may hold values from -0.125 to 0.125
- query_right: float32 [16, 2048], P(None, 'tensor'), may hold values from -0.3 to 0.3
- query_magnitude: float32 [2048], P('tensor'), may hold values from 0.5 to 2
- key_base: bfloat16 [2048, 2048], P(None, 'tensor'), may hold values from -0.125 to 0.125
- key_left: float32 [2048, 16], replicated, may hold values from -0.125 to 0.125
- key_right: float32 [16, 2048], P(None, 'tensor'), may hold values from -0.3 to 0.3
- key_magnitude: float32 [2048], P('tensor'), may hold values from 0.5 to 2
- value_base: bfloat16 [2048, 2048], P(None, 'tensor'), may hold values from -0.125 to 0.125
- value_left: float32 [2048, 16], replicated, may hold values from -0.125 to 0.125
- value_right: float32 [16, 2048], P(None, 'tensor'), may hold values from -0.3 to 0.3
- value_magnitude: float32 [2048], P('tensor'), may hold values from 0.5 to 2
- output_base: bfloat16 [2048, 2048], P('tensor'), may hold values from -0.125 to 0.125
- output_left: float32 [2048, 16], P('tensor'), may hold values from -0.125 to 0.125
- output_right: float32 [16, 2048], replicated, may hold values from -0.3 to 0.3
- output_magnitude: float32 [2048], replicated, may hold values from 3 to 12
- gate_base: bfloat16 [2048, 5632], P(None, 'tensor'), may hold values from -0.125 to 0.125
- gate_left: float32 [2048, 16], replicated, may hold values from -0.125 to 0.125
- gate_right: float32 [16, 5632], P(None, 'tensor'), may hold values from -0.3 to 0.3
- gate_magnitude: float32 [5632], P('tensor'), may hold values from 0.5 to 2
- up_base: bfloat16 [2048, 5632], P(None, 'tensor'), may hold values from -0.125 to 0.125
- up_left: float32 [2048, 16], replicated, may hold values from -0.125 to 0.125
- up_right: float32 [16, 5632], P(None, 'tensor'), may hold values from -0.3 to 0.3
- up_magnitude: float32 [5632], P('tensor'), may hold values from 0.5 to 2
- down_base: bfloat16 [5632, 2048], P('tensor'), may hold values from -0.078125 to 0.078125
- down_left: float32 [5632, 16], P('tensor'), may hold values from -0.078125 to 0.078125
- down_right: float32 [16, 2048], replicated, may hold values from -0.3 to 0.3
- down_magnitude: float32 [2048], replicated, may hold values from 1 to 4
- cotangent: bfloat16 [16, 1024, 2048], P('dp', 'tensor'), may hold values from -6 to 6
Outputs:
- layer_out: bfloat16 [16, 1024, 2048], P('dp', 'tensor')
- input_grad: float32 [16, 1024, 2048], P('dp', 'tensor')
- query_left_grad: float32 [2048, 16], replicated
- query_right_grad: float32 [16, 2048], P(None, 'tensor')
- query_magnitude_grad: float32 [2048], P('tensor')
- key_left_grad: float32 [2048, 16], replicated
- key_right_grad: float32 [16, 2048], P(None, 'tensor')
- key_magnitude_grad: float32 [2048], P('tensor')
- value_left_grad: float32 [2048, 16], replicated
- value_right_grad: float32 [16, 2048], P(None, 'tensor')
- value_magnitude_grad: float32 [2048], P('tensor')
- output_left_grad: float32 [2048, 16], P('tensor')
- output_right_grad: float32 [16, 2048], replicated
- output_magnitude_grad: float32 [2048], replicated
- gate_left_grad: float32 [2048, 16], replicated
- gate_right_grad: float32 [16, 5632], P(None, 'tensor')
- gate_magnitude_grad: float32 [5632], P('tensor')
- up_left_grad: float32 [2048, 16], replicated
- up_right_grad: float32 [16, 5632], P(None, 'tensor')
- up_magnitude_grad: float32 [5632], P('tensor')
- down_left_grad: float32 [5632, 16], P('tensor')
- down_right_grad: float32 [16, 2048], replicated
- down_magnitude_grad: float32 [2048], replicated
Inputs may be any that keep to these rules, and one draw needn't show every extreme that they name: `segment_ids`: each row holds three documents numbered 0, 1, 2 in order; document 1 begins within the first 128 positions, after position 0, and ends within the last 128 positions, before the last one.
All inputs are finite; a program needn't handle non-finite values.
Results may differ from a plain program's by a relative error of at most 0.03.
Values may be sent and summed in bfloat16 or wider, within the bound.
No kernel may reach another device: no remote copies, remote signals or barrier semaphores. Data moves between devices by JAX's collectives and lax.ppermute only.
A program may use at most 256 MiB of HBM per device.

v0:
```python
import jax
import jax.numpy as jnp
from jax import lax
from jax.sharding import Mesh
from jax.sharding import PartitionSpec as P

HEAD_DIM = 128
RANK = 16
ALPHA = 32
TENSOR = ("tensor_0", "tensor_1")
DP_TENSOR = ("dp", "tensor_0", "tensor_1")


EPSILON = 1e-05
MASKED_SCORE = -1e30
HIGHEST_PRECISION = lax.Precision.HIGHEST


def sent_to_all(array, axis):
    devices = lax.axis_size(axis)
    return lax.all_to_all(
        jnp.broadcast_to(array[None], (devices, *array.shape)), axis, 0, 0, tiled=True
    )


def of_everyone(array, axis):
    return sent_to_all(array, axis).astype(jnp.float32).sum(axis=0)


def whole_of(array, axes, dim):
    if not axes:
        return array
    nearer = lax.all_gather(array, axes[-1], axis=dim, tiled=True)
    return whole_of(nearer, axes[:-1], dim)


def precise_dot(left_side, right_side):
    return jnp.dot(
        left_side, right_side, precision=HIGHEST_PRECISION, preferred_element_type=jnp.float32
    )


def plain_dot(left_side, right_side):
    return jnp.dot(left_side, right_side, preferred_element_type=jnp.float32)


def rows_of(array, first_row, row_count):
    return lax.dynamic_slice_in_dim(array, first_row, row_count, 0)


def rms_forward(resid, gain):
    inverse = lax.rsqrt(jnp.mean(resid * resid, axis=-1, keepdims=True) + EPSILON)
    normal = resid * inverse
    return (normal, inverse, (normal * gain.astype(jnp.float32)).astype(jnp.bfloat16))


def rms_backward(grad_normed, normal, inverse, gain):
    scaled = grad_normed * gain.astype(jnp.float32)
    return inverse * (scaled - normal * jnp.mean(scaled * normal, axis=-1, keepdims=True))


def rotate_half(values):
    middle = values.shape[-1] // 2
    return jnp.concatenate([-values[..., middle:], values[..., :middle]], axis=-1)


def column_forward(inputs, base, left, right, magnitude):
    factor = ALPHA / RANK
    weight = base.astype(jnp.float32) + factor * precise_dot(left, right)
    column_norm = jnp.sqrt(jnp.sum(weight * weight, axis=0))
    lowrank = precise_dot(inputs, left)
    raw = plain_dot(inputs, base) + factor * precise_dot(lowrank, right)
    return (raw, magnitude / column_norm, lowrank, weight, column_norm)


def column_backward(grad_value, inputs, left, right, magnitude, saved):
    factor = ALPHA / RANK
    raw, scale, lowrank, weight, column_norm = saved
    scale_sum = jnp.sum(grad_value * raw, axis=0)
    coefficient = -scale_sum * magnitude / (column_norm * column_norm * column_norm)
    grad_raw = (grad_value * scale).astype(jnp.bfloat16)
    through = precise_dot(grad_raw, right.T)
    weighted = weight * coefficient
    grad_left = factor * (precise_dot(inputs.T, through) + precise_dot(weighted, right.T))
    grad_right = factor * (precise_dot(lowrank.T, grad_raw) + precise_dot(left.T, weighted))
    return (grad_raw, through, grad_left, grad_right, scale_sum / column_norm)


def on_device(
    hidden_in,
    segment_ids,
    attention_gain,
    mlp_gain,
    query_base,
    query_left,
    query_right,
    query_magnitude,
    key_base,
    key_left,
    key_right,
    key_magnitude,
    value_base,
    value_left,
    value_right,
    value_magnitude,
    output_base,
    output_left,
    output_right,
    output_magnitude,
    gate_base,
    gate_left,
    gate_right,
    gate_magnitude,
    up_base,
    up_left,
    up_right,
    up_magnitude,
    down_base,
    down_left,
    down_right,
    down_magnitude,
    cotangent,
):
    factor = ALPHA / RANK
    group_size = lax.axis_size(TENSOR)
    resid = hidden_in[0].astype(jnp.float32)
    segments = segment_ids[0]
    length = segments.shape[0]
    local_rows = resid.shape[0]
    heads_here = query_base.shape[1] // HEAD_DIM
    width_here = heads_here * HEAD_DIM
    out_weight = output_base.astype(jnp.float32) + factor * precise_dot(output_left, output_right)
    down_weight = down_base.astype(jnp.float32) + factor * precise_dot(down_left, down_right)
    out_squares, down_squares, out_cross, down_cross = (
        of_everyone(jnp.sum(out_weight * out_weight, axis=0).astype(jnp.bfloat16), TENSOR).astype(
            jnp.float32
        ),
        of_everyone(jnp.sum(down_weight * down_weight, axis=0).astype(jnp.bfloat16), TENSOR).astype(
            jnp.float32
        ),
        of_everyone(precise_dot(output_left.T, out_weight).astype(jnp.bfloat16), TENSOR).astype(
            jnp.float32
        ),
        of_everyone(precise_dot(down_left.T, down_weight).astype(jnp.bfloat16), TENSOR).astype(
            jnp.float32
        ),
    )
    out_norm = jnp.sqrt(out_squares)
    down_norm = jnp.sqrt(down_squares)
    out_scale = output_magnitude / out_norm
    down_scale = down_magnitude / down_norm
    whole_output = whole_of(output_base, TENSOR, 0)
    normal_one, inverse_one, normed_one = rms_forward(resid, attention_gain)
    gathered_one = lax.all_gather(normed_one, TENSOR, axis=0, tiled=True)
    query_saved = column_forward(gathered_one, query_base, query_left, query_right, query_magnitude)
    key_saved = column_forward(gathered_one, key_base, key_left, key_right, key_magnitude)
    value_saved = column_forward(gathered_one, value_base, value_left, value_right, value_magnitude)
    index = jnp.arange(length, dtype=jnp.int32)
    change = jnp.concatenate([jnp.ones((1,), dtype=bool), segments[1:] != segments[:-1]])
    starts = lax.cummax(jnp.where(change, index, 0), axis=0)
    positions = (index - starts).astype(jnp.float32)
    frequency = 10000.0 ** (-jnp.arange(0, HEAD_DIM, 2, dtype=jnp.float32) / HEAD_DIM)
    angles = positions[:, None] * frequency[None, :]
    cosine = jnp.concatenate([jnp.cos(angles), jnp.cos(angles)], axis=-1)[:, None, :]
    sine_table = jnp.concatenate([jnp.sin(angles), jnp.sin(angles)], axis=-1)[:, None, :]

    def rotate(values):
        return values * cosine + rotate_half(values) * sine_table

    def unrotate(grads):
        return grads * cosine - rotate_half(grads * sine_table)

    queries = rotate(
        (query_saved[0] * query_saved[1]).reshape(length, heads_here, HEAD_DIM)
    ).astype(jnp.bfloat16)
    keys = rotate((key_saved[0] * key_saved[1]).reshape(length, heads_here, HEAD_DIM)).astype(
        jnp.bfloat16
    )
    values = (
        (value_saved[0] * value_saved[1]).reshape(length, heads_here, HEAD_DIM).astype(jnp.bfloat16)
    )
    block_rows = min(512, length)
    block_count = length // block_rows
    block_starts = jnp.arange(block_count, dtype=jnp.int32) * block_rows
    score_scale = HEAD_DIM ** (-0.5)

    def block_scores(query_block, first_row):
        scores = (
            jnp.einsum("qhd,khd->hqk", query_block, keys, preferred_element_type=jnp.float32)
            * score_scale
        )
        query_index = first_row + jnp.arange(block_rows, dtype=jnp.int32)
        query_segments = rows_of(segments, first_row, block_rows)
        allowed = (query_segments[:, None] == segments[None, :]) & (
            index[None, :] <= query_index[:, None]
        )
        return jnp.where(allowed[None], scores, MASKED_SCORE)

    def forward_block(first_row):
        query_block = rows_of(queries, first_row, block_rows)
        scores = block_scores(query_block, first_row)
        largest = jnp.max(scores, axis=-1, keepdims=True)
        weights = jnp.exp(scores - largest)
        totals = jnp.sum(weights, axis=-1, keepdims=True)
        probabilities = (weights / totals).astype(jnp.bfloat16)
        attended_block = jnp.einsum(
            "hqk,khd->qhd", probabilities, values, preferred_element_type=jnp.float32
        )
        return (attended_block.astype(jnp.bfloat16), (largest + jnp.log(totals))[..., 0])

    attended_blocks, log_totals = lax.map(forward_block, block_starts)
    attended = attended_blocks.reshape(length, width_here)
    arrived, low_parts = (
        lax.all_to_all(
            attended.astype(jnp.float32).astype(jnp.bfloat16),
            TENSOR,
            split_axis=0,
            concat_axis=1,
            tiled=True,
        ).astype(jnp.float32),
        lax.all_to_all(
            precise_dot(attended, output_left).astype(jnp.bfloat16),
            TENSOR,
            split_axis=0,
            concat_axis=1,
            tiled=True,
        ).astype(jnp.float32),
    )
    attended_rows = arrived.astype(jnp.bfloat16)
    out_low = jnp.sum(low_parts.reshape(local_rows, group_size, RANK), axis=1)
    out_raw = plain_dot(attended_rows, whole_output) + factor * precise_dot(out_low, output_right)
    resid_two = resid + out_raw * out_scale
    normal_two, inverse_two, normed_two = rms_forward(resid_two, mlp_gain)
    gathered_two = lax.all_gather(normed_two, TENSOR, axis=0, tiled=True)
    gate_saved = column_forward(gathered_two, gate_base, gate_left, gate_right, gate_magnitude)
    up_saved = column_forward(gathered_two, up_base, up_left, up_right, up_magnitude)
    gate_value = gate_saved[0] * gate_saved[1]
    up_value = up_saved[0] * up_saved[1]
    sigmoid = jax.nn.sigmoid(gate_value)
    activated = (gate_value * sigmoid * up_value).astype(jnp.bfloat16)
    activated_low = precise_dot(activated, down_left)
    first_row = jnp.int32(0)
    down_raw = lax.psum_scatter(
        (
            plain_dot(rows_of(activated, first_row, local_rows * lax.axis_size(TENSOR)), down_base)
            + factor
            * precise_dot(
                rows_of(activated_low, first_row, local_rows * lax.axis_size(TENSOR)), down_right
            )
        ).astype(jnp.bfloat16),
        TENSOR,
        scatter_dimension=0,
        tiled=True,
    ).astype(jnp.float32)
    layer = resid_two + down_raw * down_scale
    grad_layer = cotangent[0].astype(jnp.float32)
    down_scale_part = jnp.sum(grad_layer * down_raw, axis=0)
    down_grad_raw = (grad_layer * down_scale).astype(jnp.bfloat16)
    down_grad_all = lax.all_gather(down_grad_raw, TENSOR, axis=0, tiled=True)
    down_through = precise_dot(down_grad_all, down_right.T)
    grad_activated = plain_dot(down_grad_all, down_base.T) + factor * precise_dot(
        down_through, down_left.T
    )
    down_left_rows = factor * precise_dot(activated.T, down_through)
    down_right_part = factor * precise_dot(activated_low.T, down_grad_all)
    grad_gate = grad_activated * up_value * sigmoid * (1.0 + gate_value * (1.0 - sigmoid))
    grad_up = grad_activated * gate_value * sigmoid
    gate_back = column_backward(
        grad_gate, gathered_two, gate_left, gate_right, gate_magnitude, gate_saved
    )
    up_back = column_backward(grad_up, gathered_two, up_left, up_right, up_magnitude, up_saved)
    first_row = jnp.int32(0)
    row_count = local_rows * lax.axis_size(TENSOR)
    gate_term = plain_dot(
        rows_of(gate_back[0], first_row, row_count), gate_base.T
    ) + factor * precise_dot(rows_of(gate_back[1], first_row, row_count), gate_left.T)
    up_term = plain_dot(
        rows_of(up_back[0], first_row, row_count), up_base.T
    ) + factor * precise_dot(rows_of(up_back[1], first_row, row_count), up_left.T)
    grad_normed_two = lax.psum_scatter(
        (gate_term + up_term).astype(jnp.bfloat16), TENSOR, scatter_dimension=0, tiled=True
    ).astype(jnp.float32)
    grad_resid_two = grad_layer + rms_backward(grad_normed_two, normal_two, inverse_two, mlp_gain)
    out_scale_part = jnp.sum(grad_resid_two * out_raw, axis=0)
    out_grad_raw = (grad_resid_two * out_scale).astype(jnp.bfloat16)
    out_through_rows = precise_dot(out_grad_raw, output_right.T)
    base_part = plain_dot(out_grad_raw, whole_output.T)
    head_part, out_through = (
        lax.all_to_all(
            base_part.astype(jnp.bfloat16), TENSOR, split_axis=1, concat_axis=0, tiled=True
        ).astype(base_part.dtype),
        lax.all_to_all(
            jnp.tile(out_through_rows, (1, group_size)).astype(jnp.bfloat16),
            TENSOR,
            split_axis=1,
            concat_axis=0,
            tiled=True,
        ).astype(jnp.float32),
    )
    grad_attended = (head_part + factor * precise_dot(out_through, output_left.T)).astype(
        jnp.bfloat16
    )
    out_right_part = factor * precise_dot(out_low.T, out_grad_raw)
    out_left_rows = factor * precise_dot(attended.T, out_through)
    grad_heads = grad_attended.reshape(length, heads_here, HEAD_DIM)

    def backward_block(carry, block_inputs):
        grad_keys, grad_values = carry
        first_row, log_block = block_inputs
        query_block = rows_of(queries, first_row, block_rows)
        grad_block = rows_of(grad_heads, first_row, block_rows)
        scores = block_scores(query_block, first_row)
        probabilities = jnp.exp(scores - log_block[..., None])
        grad_values = grad_values + jnp.einsum(
            "hqk,qhd->khd",
            probabilities.astype(jnp.bfloat16),
            grad_block,
            preferred_element_type=jnp.float32,
        )
        grad_probs = jnp.einsum(
            "qhd,khd->hqk", grad_block, values, preferred_element_type=jnp.float32
        )
        inner_sum = jnp.sum(grad_probs * probabilities, axis=-1, keepdims=True)
        grad_scores = (probabilities * (grad_probs - inner_sum) * score_scale).astype(jnp.bfloat16)
        grad_query_block = jnp.einsum(
            "hqk,khd->qhd", grad_scores, keys, preferred_element_type=jnp.float32
        )
        grad_keys = grad_keys + jnp.einsum(
            "hqk,qhd->khd", grad_scores, query_block, preferred_element_type=jnp.float32
        )
        return ((grad_keys, grad_values), grad_query_block)

    empty_heads = jnp.zeros((length, heads_here, HEAD_DIM), jnp.float32)
    (grad_keys, grad_values), grad_query_blocks = lax.scan(
        backward_block, (empty_heads, empty_heads), (block_starts, log_totals)
    )
    grad_queries = unrotate(grad_query_blocks.reshape(length, heads_here, HEAD_DIM)).reshape(
        length, width_here
    )
    grad_keys = unrotate(grad_keys).reshape(length, width_here)
    grad_values = grad_values.reshape(length, width_here)
    query_back = column_backward(
        grad_queries, gathered_one, query_left, query_right, query_magnitude, query_saved
    )
    key_back = column_backward(
        grad_keys, gathered_one, key_left, key_right, key_magnitude, key_saved
    )
    value_back = column_backward(
        grad_values, gathered_one, value_left, value_right, value_magnitude, value_saved
    )
    first_row = jnp.int32(0)
    row_count = local_rows * lax.axis_size(TENSOR)
    query_term = plain_dot(
        rows_of(query_back[0], first_row, row_count), query_base.T
    ) + factor * precise_dot(rows_of(query_back[1], first_row, row_count), query_left.T)
    key_term = plain_dot(
        rows_of(key_back[0], first_row, row_count), key_base.T
    ) + factor * precise_dot(rows_of(key_back[1], first_row, row_count), key_left.T)
    value_term = plain_dot(
        rows_of(value_back[0], first_row, row_count), value_base.T
    ) + factor * precise_dot(rows_of(value_back[1], first_row, row_count), value_left.T)
    grad_normed_one = lax.psum_scatter(
        (query_term + key_term + value_term).astype(jnp.bfloat16),
        TENSOR,
        scatter_dimension=0,
        tiled=True,
    ).astype(jnp.float32)
    input_grad = grad_resid_two + rms_backward(
        grad_normed_one, normal_one, inverse_one, attention_gain
    )
    shared = lax.psum(
        (
            query_back[2],
            key_back[2],
            value_back[2],
            gate_back[2],
            up_back[2],
            out_right_part,
            down_right_part,
            out_scale_part,
            down_scale_part,
        ),
        DP_TENSOR,
    )
    split_sums = (
        of_everyone(query_back[3].astype(jnp.bfloat16), "dp").astype(jnp.float32),
        of_everyone(query_back[4].astype(jnp.bfloat16), "dp").astype(jnp.float32),
        of_everyone(key_back[3].astype(jnp.bfloat16), "dp").astype(jnp.float32),
        of_everyone(key_back[4].astype(jnp.bfloat16), "dp").astype(jnp.float32),
        of_everyone(value_back[3].astype(jnp.bfloat16), "dp").astype(jnp.float32),
        of_everyone(value_back[4].astype(jnp.bfloat16), "dp").astype(jnp.float32),
        of_everyone(out_left_rows.astype(jnp.bfloat16), "dp").astype(jnp.float32),
        of_everyone(gate_back[3].astype(jnp.bfloat16), "dp").astype(jnp.float32),
        of_everyone(gate_back[4].astype(jnp.bfloat16), "dp").astype(jnp.float32),
        of_everyone(up_back[3].astype(jnp.bfloat16), "dp").astype(jnp.float32),
        of_everyone(up_back[4].astype(jnp.bfloat16), "dp").astype(jnp.float32),
        of_everyone(down_left_rows.astype(jnp.bfloat16), "dp").astype(jnp.float32),
    )
    out_coefficient = -shared[7] * output_magnitude / (out_norm * out_norm * out_norm)
    down_coefficient = -shared[8] * down_magnitude / (down_norm * down_norm * down_norm)
    out_right_grad = shared[5] + factor * out_cross * out_coefficient[None, :]
    down_right_grad = shared[6] + factor * down_cross * down_coefficient[None, :]
    out_left_grad = split_sums[6] + factor * precise_dot(
        out_weight * out_coefficient, output_right.T
    )
    down_left_grad = split_sums[11] + factor * precise_dot(
        down_weight * down_coefficient, down_right.T
    )
    return (
        layer.astype(jnp.bfloat16)[None],
        input_grad[None],
        shared[0],
        split_sums[0],
        split_sums[1],
        shared[1],
        split_sums[2],
        split_sums[3],
        shared[2],
        split_sums[4],
        split_sums[5],
        out_left_grad,
        out_right_grad,
        shared[7] / out_norm,
        shared[3],
        split_sums[7],
        split_sums[8],
        shared[4],
        split_sums[9],
        split_sums[10],
        down_left_grad,
        down_right_grad,
        shared[8] / down_norm,
    )


def solution(mesh):
    torus = Mesh(mesh.devices.reshape(mesh.shape["dp"], 4, 2), ("dp", "tensor_0", "tensor_1"))
    return jax.shard_map(
        on_device,
        mesh=torus,
        in_specs=(
            P("dp", TENSOR, None),
            P("dp", None),
            P(),
            P(),
            P(None, TENSOR),
            P(),
            P(None, TENSOR),
            P(TENSOR),
            P(None, TENSOR),
            P(),
            P(None, TENSOR),
            P(TENSOR),
            P(None, TENSOR),
            P(),
            P(None, TENSOR),
            P(TENSOR),
            P(TENSOR, None),
            P(TENSOR, None),
            P(),
            P(),
            P(None, TENSOR),
            P(),
            P(None, TENSOR),
            P(TENSOR),
            P(None, TENSOR),
            P(),
            P(None, TENSOR),
            P(TENSOR),
            P(TENSOR, None),
            P(TENSOR, None),
            P(),
            P(),
            P("dp", TENSOR, None),
        ),
        out_specs=(
            P("dp", TENSOR, None),
            P("dp", TENSOR, None),
            P(),
            P(None, TENSOR),
            P(TENSOR),
            P(),
            P(None, TENSOR),
            P(TENSOR),
            P(),
            P(None, TENSOR),
            P(TENSOR),
            P(TENSOR, None),
            P(),
            P(),
            P(),
            P(None, TENSOR),
            P(TENSOR),
            P(),
            P(None, TENSOR),
            P(TENSOR),
            P(TENSOR, None),
            P(),
            P(),
        ),
        check_vma=False,
    )
```

profile of v0, /device:TPU:1, one launch (start us, length us, event | category | flops | bytes accessed | tf_op | source)
XLA Modules:
  0.0 1167.9 jit_solution(15044461823254771933)
XLA Ops:
  12.6 36.0 %all-gather.8.cloned.1.call-done = bf16[512,2048]{1,0:T(8,128)(2,1)} async-done(((bf16[256,2048]{1,0:T(8,128)(2,1)}), bf16[512,2048]{1,0:T(8,128)(2,1)}) %all-gather.8.cloned.1.call-update) | async-done | bytes 2097168 | tf_op jit(solution)/shard_map/all_gather | solution.py:33
  48.7 8.7 multiply_reduce_fusion.1
  92.0 51.2 %all-gather.6.cloned.1.call-done = bf16[1024,2048]{1,0:T(8,128)(2,1)} async-done(((bf16[128,2048]{1,0:T(8,128)(2,1)}), bf16[1024,2048]{1,0:T(8,128)(2,1)}) %all-gather.6.cloned.1.call-update) | async-done | bytes 4194320 | tf_op jit(solution)/shard_map/all_gather | solution.py:154
  177.8 19.9 %while.28 = (s32[]{:T(128)}, bf16[2,512,2,128]{3,2,1,0:T(2,128)(2,1)}, f32[2,2,512]{2,1,0:T(2,128)S(1)}, s32[2]{0:T(128)S(1)}, s32[1024]{0:T(1024)S(1)}, /*index...) while((s32[]{:T(128)}, ...), condition=%wide.region_9.0_spmd.clone, body=%wide.region_6.9_spmd.clone.sunk | while | flops 551157248 | bytes 21018872 | solution.py:211
  213.5 10.5 all-to-all-done
  224.2 10.0 all-gather.10.cloned.1.call-done
  242.4 8.8 multiply_reduce_fusion.3
  251.3 7.6 multiply_reduce_fusion.2
  258.9 68.4 %all-gather.14.cloned.1.call-done = bf16[1024,2048]{1,0:T(8,128)(2,1)} async-done(((bf16[128,2048]{1,0:T(8,128)(2,1)}), bf16[1024,2048]{1,0:T(8,128)(2,1)}) %all-gather.14.cloned.1.call-update) | async-done | bytes 4194320 | tf_op jit(solution)/shard_map/all_gather | solution.py:259
  342.3 77.9 %all-gather.12.cloned.1.call-done = bf16[1024,2048]{1,0:T(8,128)(2,1)} async-done(((bf16[128,2048]{1,0:T(8,128)(2,1)}), bf16[1024,2048]{1,0:T(8,128)(2,1)}) %all-gather.12.cloned.1.call-update) | async-done | bytes 4194320 | tf_op jit(solution)/shard_map/all_gather | solution.py:234
  466.7 12.8 %add_convert_fusion.1 = bf16[1024,2048]{1,0:T(8,128)(2,1)} fusion(f32[1024,2048]{1,0:T(8,128)S(1)} %fusion.241, f32[1024,2048]{1,0:T(8,128)} %fusion.238, f32[1024,2048]{1,0:T(8,128)S(1)} %fusion.240, f32[1024,16]{0,1:T(8,128)S(1)} %fusion.242, f32[2048,16]{0,1:T(8,128)S(1)} %copy-done.36), kind=kOutput, calls=%fused_computation.55 | convolution fusion | flops 415236096 | bytes 29556736 | tf_op jit(solution)/shard_map/dot_general | solution.py:38
  487.4 8.8 add_convert_fusion.2
  517.3 53.6 %reduce-scatter.6.cloned.1.call-done = bf16[128,2048]{1,0:T(8,128)(2,1)} async-done(((bf16[1024,2048]{1,0:T(8,128)(2,1)}), bf16[128,2048]{1,0:T(8,128)(2,1)}) %reduce-scatter.6.cloned.1.call-update) | async-done | bytes 524304 | tf_op jit(solution)/shard_map/reduce_scatter | solution.py:280
  572.8 91.8 %reduce-scatter.4.cloned.1.call-done = bf16[128,2048]{1,0:T(8,128)(2,1)} async-done(((bf16[1024,2048]{1,0:T(8,128)(2,1)}), bf16[128,2048]{1,0:T(8,128)(2,1)}) %reduce-scatter.4.cloned.1.call-update) | async-done | bytes 524304 | tf_op jit(solution)/shard_map/reduce_scatter | solution.py:243
  699.8 56.0 %while.29 = (s32[]{:T(128)}, f32[1024,2,128]{0,2,1:T(8,128)}, f32[1024,2,128]{0,2,1:T(8,128)S(1)}, f32[2,512,2,128]{3,1,2,0:T(8,128)}, s32[2]{0:T(128)S(1)}, /*i...) while((s32[]{:T(128)}, f32[1024,2,128]{0,2,1:T(8,128)}, ...), condition=%wide.region_23.24_spmd.clone, body=%wide.region_21.23_spmd.clone.sunk | while | flops 1359483392 | bytes 71330056 | solution.py:334
  711.5 8.2 fusion.443
  719.7 8.0 fusion.445
  739.3 8.5 fusion.443
  747.8 8.0 fusion.445
  795.8 9.1 fusion.248
  804.9 9.3 fusion.245
  827.4 20.3 %add_convert_fusion = bf16[1024,2048]{1,0:T(8,128)(2,1)} fusion(f32[1024,2048]{1,0:T(8,128)} %fusion.249, f32[1024,2048]{1,0:T(8,128)} %fusion.246, f32[1024,2048]{1,0:T(8,128)} %fusion.248, f32[1024,2048]{1,0:T(8,128)} %fusion.243, f32[1024,2048]{1,0:T(8,128)} %fusion.245, f32[1024,16]{0,1:T(8,128)} %copy-done.63, f32[2048,16]{0,1:T(8,128)} %param.50), kind=kOutput, calls=%fused_computation.54 | convolution fusion | flops 421527552 | bytes 46333952 | tf_op jit(solution)/shard_map/dot_general | solution.py:38
  883.4 11.6 all-to-all-start.17
  895.0 7.2 fusion.119
  905.6 7.2 all-to-all-start.15
  925.3 7.1 fusion.122
  961.4 7.2 all-to-all-done.16
  970.2 64.4 %all-reduce = (f32[2048]{0:T(1024)}, f32[2048]{0:T(1024)S(1)}) all-reduce(f32[2048]{0:T(1024)S(1)} %copy-done.111, f32[2048]{0:T(1024)S(1)} %copy-done.112), channel_id=1, replica_groups=mesh['dp'=16,'tensor_0'=4,'tensor_1'=2] {'dp','tensor_0','tensor_1'}, use_global_device_ids=true, to_apply=%region_40.41 | all-reduce | flops 4096 | bytes 32768 | tf_op jit(solution)/shard_map/psum | solution.py:371
  1035.2 7.7 fusion.128
  1050.7 7.8 all-to-all-done.12
  1082.4 7.3 all-to-all-start.7
  1097.5 7.2 all-to-all-start.9
  (593 shorter events, 491.9 us)
Async XLA Ops:
  7.2 41.4 %all-gather.8.cloned.1.call-start = ((), (), s32[]{:S(2)}) async-start(), calls=%async_computation.24 | async-start | bytes 3145728 | tf_op jit(solution)/shard_map/all_gather | solution.py:33
  8.0 135.3 %all-gather.6.cloned.1.call-start = ((), (), s32[]{:S(2)}) async-start(), calls=%async_computation.23 | async-start | bytes 4718592 | tf_op jit(solution)/shard_map/all_gather | solution.py:154
  12.5 221.7 %all-gather.10.cloned.1.call-start = ((), (), s32[]{:S(2)}) async-start(), calls=%async_computation.25 | async-start | bytes 10485760 | tf_op jit(solution)/shard_map/all_gather | solution.py:33
  59.4 26.2 %all-to-all-start.3 = ((bf16[8,2,1024]{2,1,0:T(2,128)(2,1)}), bf16[8,2,1024]{2,1,0:T(2,128)(2,1)S(1)}, u32[]{:S(2)}, u32[]{:S(2)}) async-start(bf16[8,2,1024]{2,1,0:T(2,128)(2,1)} %reshape.443), calls=%async_computation.4 | async-start | bytes 65536 | tf_op jit(solution)/shard_map/all_to_all | solution.py:21
  80.2 91.3 %copy-start.119 = (f32[256]{0:T(256)}, f32[256]{0:T(256)S(1)}, u32[]{:S(2)}) copy-start(f32[256]{0:T(256)S(1)} %sqrt_divide_fusion.6) | copy-start | bytes 3076
  85.6 114.3 %all-to-all-start.2 = ((bf16[8,2,1024]{2,1,0:T(2,128)(2,1)}), bf16[8,2,1024]{2,1,0:T(2,128)(2,1)}, u32[]{:S(2)}, u32[]{:S(2)}) async-start(bf16[8,2,1024]{2,1,0:T(2,128)(2,1)} %reshape.441), calls=%async_computation.2 | async-start | bytes 65536 | tf_op jit(solution)/shard_map/all_to_all | solution.py:21
  90.7 236.6 %all-gather.14.cloned.1.call-start = ((), (), s32[]{:S(2)}) async-start(), calls=%async_computation.28 | async-start | bytes 4718592 | tf_op jit(solution)/shard_map/all_gather | solution.py:259
  199.9 8.5 all-to-all-start.1
  208.4 15.6 %all-to-all-start = ((bf16[8,128,256]{2,1,0:T(8,128)(2,1)}), bf16[8,128,256]{2,1,0:T(8,128)(2,1)S(1)}, u32[]{:S(2)}, u32[]{:S(2)}) async-start(bf16[8,128,256]{2,1,0:T(8,128)(2,1)} %all_to_all.101), calls=%async_computation | async-start | bytes 1048576 | tf_op jit(solution)/shard_map/all_to_all | solution.py:214
  211.9 208.3 %all-gather.12.cloned.1.call-start = ((), (), s32[]{:S(2)}) async-start(), calls=%async_computation.26 | async-start | bytes 4718592 | tf_op jit(solution)/shard_map/all_gather | solution.py:234
  242.3 328.6 %reduce-scatter.6.cloned.1.call-start = ((), (), s32[]{:S(2)}) async-start(), calls=%async_computation.29 | async-start | bytes 4718592 | tf_op jit(solution)/shard_map/reduce_scatter | solution.py:280
  479.5 185.1 %reduce-scatter.4.cloned.1.call-start = ((), (), s32[]{:S(2)}) async-start(), calls=%async_computation.27 | async-start | bytes 4718592 | tf_op jit(solution)/shard_map/reduce_scatter | solution.py:243
  670.6 13.6 %all-to-all-start.5 = ((bf16[128,8,16]{0,2,1:T(8,128)(2,1)}), bf16[128,8,16]{0,2,1:T(8,128)(2,1)}, u32[]{:S(2)}, u32[]{:S(2)}) async-start(bf16[128,8,16]{0,2,1:T(8,128)(2,1)} %tile.2), calls=%async_computation.7 | async-start | bytes 65536 | tf_op jit(solution)/shard_map/all_to_all | solution.py:292
  684.2 13.9 %all-to-all-start.4 = ((bf16[128,8,256]{0,2,1:T(8,128)(2,1)}), bf16[128,8,256]{0,2,1:T(8,128)(2,1)}, u32[]{:S(2)}, u32[]{:S(2)}) async-start(bf16[128,8,256]{0,2,1:T(8,128)(2,1)} %bitcast.343), calls=%async_computation.6 | async-start | bytes 1048576 | tf_op jit(solution)/shard_map/all_to_all | solution.py:289
  689.3 461.2 %all-reduce.4.cloned.1.call-start = ((), (), s32[]{:S(2)}) async-start(), calls=%async_computation.31 | async-start | bytes 1835008 | tf_op jit(solution)/shard_map/psum | solution.py:371
  827.3 326.4 %reduce-scatter.8.cloned.1.call-start = ((), (), s32[]{:S(2)}) async-start(), calls=%async_computation.30 | async-start | bytes 4718592 | tf_op jit(solution)/shard_map/reduce_scatter | solution.py:362
  852.0 11.9 %all-to-all-start.13 = ((bf16[8,16,2048]{2,1,0:T(8,128)(2,1)}), bf16[8,16,2048]{2,1,0:T(8,128)(2,1)}, u32[]{:S(2)}, u32[]{:S(2)}) async-start(bf16[8,16,2048]{2,1,0:T(8,128)(2,1)} %broadcast_in_dim.106), calls=%async_computation.16 | async-start | bytes 1048576 | tf_op jit(solution)/shard_map/all_to_all | solution.py:21
  865.6 11.9 %all-to-all-start.19 = ((bf16[8,16,2048]{2,1,0:T(8,128)(2,1)}), bf16[8,16,2048]{2,1,0:T(8,128)(2,1)}, u32[]{:S(2)}, u32[]{:S(2)}) async-start(bf16[8,16,2048]{2,1,0:T(8,128)(2,1)} %broadcast_in_dim.112), calls=%async_computation.22 | async-start | bytes 1048576 | tf_op jit(solution)/shard_map/all_to_all | solution.py:21
  883.4 22.2 %all-to-all-start.17 = ((bf16[16,2,352]{2,1,0:T(2,128)(2,1)}), bf16[16,2,352]{2,1,0:T(2,128)(2,1)}, u32[]{:S(2)}, u32[]{:S(2)}) async-start(bf16[16,2,352]{2,1,0:T(2,128)(2,1)} %reshape.453), calls=%async_computation.20 | async-start | bytes 49152 | tf_op jit(solution)/shard_map/all_to_all | solution.py:21
  905.6 14.5 %all-to-all-start.15 = ((bf16[16,2,352]{2,1,0:T(2,128)(2,1)}), bf16[16,2,352]{2,1,0:T(2,128)(2,1)S(1)}, u32[]{:S(2)}, u32[]{:S(2)}) async-start(bf16[16,2,352]{2,1,0:T(2,128)(2,1)} %reshape.451), calls=%async_computation.18 | async-start | bytes 49152 | tf_op jit(solution)/shard_map/all_to_all | solution.py:21
  920.9 14.4 %all-to-all-start.18 = ((bf16[16,704,16]{1,2,0:T(8,128)(2,1)}), bf16[16,704,16]{1,2,0:T(8,128)(2,1)}, u32[]{:S(2)}, u32[]{:S(2)}) async-start(bf16[16,704,16]{1,2,0:T(8,128)(2,1)} %broadcast_in_dim.111), calls=%async_computation.21 | async-start | bytes 786432 | tf_op jit(solution)/shard_map/all_to_all | solution.py:21
  932.4 102.2 %copy-start.102 = (f32[2048]{0:T(1024)S(1)}, f32[2048]{0:T(1024)}, u32[]{:S(2)}) copy-start(f32[2048]{0:T(1024)} %copy-done.101) | copy-start | bytes 24580
  932.5 102.1 %copy-start.114 = (f32[2048]{0:T(1024)S(1)}, f32[2048]{0:T(1024)}, u32[]{:S(2)}) copy-start(f32[2048]{0:T(1024)} %param.68) | copy-start | bytes 24580
  936.9 15.2 %all-to-all-start.14 = ((bf16[16,16,704]{2,1,0:T(8,128)(2,1)}), bf16[16,16,704]{2,1,0:T(8,128)(2,1)}, u32[]{:S(2)}, u32[]{:S(2)}) async-start(bf16[16,16,704]{2,1,0:T(8,128)(2,1)} %broadcast_in_dim.107), calls=%async_computation.17 | async-start | bytes 786432 | tf_op jit(solution)/shard_map/all_to_all | solution.py:21
  952.9 15.6 %all-to-all-start.16 = ((bf16[16,16,704]{2,1,0:T(8,128)(2,1)}), bf16[16,16,704]{2,1,0:T(8,128)(2,1)}, u32[]{:S(2)}, u32[]{:S(2)}) async-start(bf16[16,16,704]{2,1,0:T(8,128)(2,1)} %broadcast_in_dim.109), calls=%async_computation.19 | async-start | bytes 786432 | tf_op jit(solution)/shard_map/all_to_all | solution.py:21
  1044.5 14.1 %all-to-all-start.12 = ((bf16[16,256,16]{1,2,0:T(8,128)(2,1)}), bf16[16,256,16]{1,2,0:T(8,128)(2,1)}, u32[]{:S(2)}, u32[]{:S(2)}) async-start(bf16[16,256,16]{1,2,0:T(8,128)(2,1)} %broadcast_in_dim.105), calls=%async_computation.15 | async-start | bytes 262144 | tf_op jit(solution)/shard_map/all_to_all | solution.py:21
  1066.7 15.8 %all-to-all-start.11 = ((bf16[16,2,128]{2,1,0:T(2,128)(2,1)}), bf16[16,2,128]{2,1,0:T(2,128)(2,1)}, u32[]{:S(2)}, u32[]{:S(2)}) async-start(bf16[16,2,128]{2,1,0:T(2,128)(2,1)} %reshape.449), calls=%async_computation.14 | async-start | bytes 16384 | tf_op jit(solution)/shard_map/all_to_all | solution.py:21
  1082.4 15.1 %all-to-all-start.7 = ((bf16[16,2,128]{2,1,0:T(2,128)(2,1)}), bf16[16,2,128]{2,1,0:T(2,128)(2,1)}, u32[]{:S(2)}, u32[]{:S(2)}) async-start(bf16[16,2,128]{2,1,0:T(2,128)(2,1)} %reshape.445), calls=%async_computation.10 | async-start | bytes 16384 | tf_op jit(solution)/shard_map/all_to_all | solution.py:21
  1097.5 14.2 %all-to-all-start.9 = ((bf16[16,2,128]{2,1,0:T(2,128)(2,1)}), bf16[16,2,128]{2,1,0:T(2,128)(2,1)}, u32[]{:S(2)}, u32[]{:S(2)}) async-start(bf16[16,2,128]{2,1,0:T(2,128)(2,1)} %reshape.447), calls=%async_computation.12 | async-start | bytes 16384 | tf_op jit(solution)/shard_map/all_to_all | solution.py:21
  1112.4 12.0 %all-to-all-start.10 = ((bf16[16,16,256]{2,1,0:T(8,128)(2,1)}), bf16[16,16,256]{2,1,0:T(8,128)(2,1)S(1)}, u32[]{:S(2)}, u32[]{:S(2)}) async-start(bf16[16,16,256]{2,1,0:T(8,128)(2,1)} %broadcast_in_dim.103), calls=%async_computation.13 | async-start | bytes 262144 | tf_op jit(solution)/shard_map/all_to_all | solution.py:21
  1125.7 11.7 %all-to-all-start.6 = ((bf16[16,16,256]{2,1,0:T(8,128)(2,1)}), bf16[16,16,256]{2,1,0:T(8,128)(2,1)S(1)}, u32[]{:S(2)}, u32[]{:S(2)}) async-start(bf16[16,16,256]{2,1,0:T(8,128)(2,1)} %broadcast_in_dim.99), calls=%async_computation.9 | async-start | bytes 262144 | tf_op jit(solution)/shard_map/all_to_all | solution.py:21
  1138.1 11.7 %all-to-all-start.8 = ((bf16[16,16,256]{2,1,0:T(8,128)(2,1)}), bf16[16,16,256]{2,1,0:T(8,128)(2,1)S(1)}, u32[]{:S(2)}, u32[]{:S(2)}) async-start(bf16[16,16,256]{2,1,0:T(8,128)(2,1)} %broadcast_in_dim.101), calls=%async_computation.11 | async-start | bytes 262144 | tf_op jit(solution)/shard_map/all_to_all | solution.py:21
  (149 other events, 2044.6 us)
Sparse Core Ops, SparseCore 0:
  9.7 38.8 all-gather.7
  50.8 92.3 all-gather.5
  144.9 89.3 all-gather.9
  235.7 91.5 all-gather.13
  329.4 90.7 all-gather.11
  479.6 91.2 reduce-scatter.5
  573.4 91.2 reduce-scatter.3
  827.4 152.0 all-reduce.3
  982.1 91.2 reduce-scatter.7
where the time goes:
time: 1180 us; the launch traced here: 1170 us
  waiting for transfers between devices  462 us (39%)
  matrix products  369 us (31%)
  starting transfers between devices  105 us (9%)
  other arithmetic  78.6 us (7%)
  local copies, waits for them, and re-layouts  65.3 us (6%)
  blocking collectives  64.4 us (5%)
  between operations  15.8 us (1%)
    dot_general x63, matrix products, precise_dot(): jnp.dot(left_side, right_side, precision=HIGHEST_PRECISION, preferred_ele...  258 us
    reduce_scatter x1, waiting for transfers between devices, on_device(): lax.psum_scatter((plain_dot(rows_of(activated, first_row, local_rows * la...  91.8 us
    all_to_all x16, starting transfers between devices, sent_to_all(): lax.all_to_all(jnp.broadcast_to(array[None], (devices, *array.shape)), ax...  87.9 us
    all_gather x1, waiting for transfers between devices, on_device(): gathered_two = lax.all_gather(normed_two, TENSOR, axis=0, tiled=True)  77.9 us
    all_gather x1, waiting for transfers between devices, on_device(): down_grad_all = lax.all_gather(down_grad_raw, TENSOR, axis=0, tiled=True)  68.4 us
    psum x1, blocking collectives, on_device(): lax.psum((query_back[2], key_back[2], value_back[2], gate_back[2], up_bac...  64.4 us
    dot_general x14, matrix products, plain_dot(): return jnp.dot(left_side, right_side, preferred_element_type=jnp.float32)  59.9 us
    all_to_all x16, waiting for transfers between devices, sent_to_all(): lax.all_to_all(jnp.broadcast_to(array[None], (devices, *array.shape)), ax...  56.1 us
  transfers between devices with their start and end apart: 29, of which 21 were waited for; matrix products, arithmetic and copies ran while one was open for 26% of the time, Pallas kernels for 0%

commit v1 on v0

v1 whole, which is shorter than its diff:
```python
import jax
import jax.numpy as jnp
from jax import lax
from jax.experimental import pallas as pl
from jax.experimental.pallas import tpu as pltpu
from jax.sharding import Mesh
from jax.sharding import PartitionSpec as P

HEAD_DIM = 128
RANK = 16
ALPHA = 32
FACTOR = ALPHA / RANK
EPSILON = 1e-05
MASKED_SCORE = -1e30
DP = ("y", "xh", "core")
TENSOR = ("z", "xl")
ALL = DP + TENSOR
BF16 = jnp.bfloat16
F32 = jnp.float32

SWAP = ((0, 1), (1, 0))
UP = tuple((i, (i + 1) % 4) for i in range(4))
DOWN = tuple((i, (i + 3) % 4) for i in range(4))
SLOTS = ((0, 0), (0, 1), (-1, 0), (1, 0), (-1, 1), (1, 1), (2, 0), (2, 1))
SLOT_AT = ((0, 1), (3, 5), (6, 7), (2, 4))


def z_up(array):
    return lax.ppermute(array, "z", UP)


def z_down(array):
    return lax.ppermute(array, "z", DOWN)


def x_swap(array):
    return lax.ppermute(array, "xl", SWAP)


def core_swap(array):
    return lax.ppermute(array, "core", SWAP)


def from_x_neighbour(array):
    pairs = []
    for x in range(4):
        for core in range(2):
            source = (x ^ 1) if core else (x + 3 if x % 2 == 0 else x + 1) % 4
            pairs.append(
                ((source // 2) * 4 + core * 2 + source % 2, (x // 2) * 4 + core * 2 + x % 2)
            )
    return lax.ppermute(array, ("xh", "core", "xl"), tuple(pairs))


def gather_row(own):
    other = x_swap(own)
    below, above = z_up(own), z_down(own)
    other_below, other_above = z_up(other), z_down(other)
    far = z_up(below)
    other_far = z_down(other_above)
    return [own, other, below, above, other_below, other_above, far, other_far]


def add(*terms):
    total = terms[0].astype(F32)
    for term in terms[1:]:
        total = total + term.astype(F32)
    return total


def scatter_row(parts):
    far = z_up(parts[6])
    other_far = z_down(parts[7])
    from_above = z_down(parts[2])
    other_from_below = z_up(parts[5])
    from_below = z_up(add(parts[3], far).astype(BF16))
    other_from_above = z_down(add(parts[4], other_far).astype(BF16))
    across = x_swap(add(parts[1], other_from_below, other_from_above).astype(BF16))
    return add(parts[0], from_below, from_above, across)


def gather_z(own):
    half = own.shape[0] // 2
    below, above = z_up(own), z_down(own)
    far_low = z_up(below[:half])
    far_high = z_down(above[half:])
    return jnp.concatenate([own, below, above, far_low, far_high], axis=0)


def scatter_z(total, rows):
    half = rows // 2
    own, below, above, far = (total[i * rows : (i + 1) * rows] for i in range(4))
    low = z_up(far[:half])
    high = z_down(far[half:])
    above_sum = jnp.concatenate([add(above[:half], low).astype(BF16), above[half:]], axis=0)
    below_sum = jnp.concatenate([below[:half], add(below[half:], high).astype(BF16)], axis=0)
    return add(own, z_up(above_sum), z_down(below_sum))


def all_to_all(array, axes):
    return lax.all_to_all(array, axes, 0, 0, tiled=True)


def of_everyone(array, axes):
    count = lax.axis_size(axes)
    return all_to_all(jnp.broadcast_to(array[None], (count, *array.shape)), axes)


def summed(arrays, axes):
    count = lax.axis_size(axes)
    flat = jnp.concatenate([a.astype(BF16).reshape(-1) for a in arrays])
    size = flat.shape[0]
    step = count * 128
    padded = (size + step - 1) // step * step
    flat = jnp.pad(flat, (0, padded - size)).reshape(count, padded // step, 128)
    part = all_to_all(flat, axes).astype(F32).sum(axis=0).astype(BF16)
    whole = of_everyone(part, axes).reshape(-1).astype(F32)
    sums, at = [], 0
    for a in arrays:
        sums.append(whole[at : at + a.size].reshape(a.shape))
        at += a.size
    return sums


def dot(left, right):
    return jnp.dot(left.astype(BF16), right.astype(BF16), preferred_element_type=F32)


def dot_nt(left, right):
    return lax.dot_general(
        left.astype(BF16), right.astype(BF16), (((1,), (1,)), ((), ())), preferred_element_type=F32
    )


def dot_tn(left, right):
    return lax.dot_general(
        left.astype(BF16), right.astype(BF16), (((0,), (0,)), ((), ())), preferred_element_type=F32
    )


def rms_forward(resid, gain):
    inverse = lax.rsqrt(jnp.mean(resid * resid, axis=-1, keepdims=True) + EPSILON)
    normal = resid * inverse
    return normal, inverse, (normal * gain.astype(F32)).astype(BF16)


def rms_backward(grad_normed, normal, inverse, gain):
    scaled = grad_normed * gain.astype(F32)
    return inverse * (scaled - normal * jnp.mean(scaled * normal, axis=-1, keepdims=True))


def rotate_half(values):
    middle = values.shape[-1] // 2
    return jnp.concatenate([-values[..., middle:], values[..., :middle]], axis=-1)


def adapted_weight(base, left, right):
    weight = base.astype(F32) + FACTOR * dot(left, right)
    return weight.astype(BF16), jnp.sum(weight * weight, axis=0)


VMEM = pl.BlockSpec(memory_space=pltpu.VMEM)
SMEM = pl.BlockSpec(memory_space=pltpu.SMEM)
QUERY_ROWS = 256
SCORE_SCALE = HEAD_DIM ** (-0.5)


def masked_scores(query, key, first_row, seg_rows, seg_cols):
    scores = lax.dot_general(
        query, key, (((1,), (1,)), ((), ())), preferred_element_type=F32
    ) * SCORE_SCALE
    row = first_row + lax.broadcasted_iota(jnp.int32, scores.shape, 0)
    column = lax.broadcasted_iota(jnp.int32, scores.shape, 1)
    allowed = (seg_rows == seg_cols) & (column <= row)
    return jnp.where(allowed, scores, MASKED_SCORE)


def attend_kernel(slot_ref, seg_row_ref, seg_col_ref, qkv_ref, out_ref, log_ref, held):
    length = held.shape[0]
    width = out_ref.shape[1]
    for block in range(length // 128):
        held[block * 128 : (block + 1) * 128, :] = qkv_ref[slot_ref[block]]
    for head in range(width // HEAD_DIM):
        at = slice(head * HEAD_DIM, (head + 1) * HEAD_DIM)
        key_at = slice(width + head * HEAD_DIM, width + (head + 1) * HEAD_DIM)
        value_at = slice(2 * width + head * HEAD_DIM, 2 * width + (head + 1) * HEAD_DIM)
        for first in range(0, length, QUERY_ROWS):
            last = first + QUERY_ROWS
            scores = masked_scores(
                held[first:last, at],
                held[:last, key_at],
                first,
                seg_row_ref[first:last, :],
                seg_col_ref[:, :last],
            )
            largest = jnp.max(scores, axis=-1, keepdims=True)
            weights = jnp.exp(scores - largest)
            totals = jnp.sum(weights, axis=-1, keepdims=True)
            probs = (weights * (1.0 / totals)).astype(BF16)
            out = jnp.dot(probs, held[:last, value_at], preferred_element_type=F32)
            out_ref[first:last, at] = out.astype(BF16)
            log_ref[first:last, at] = jnp.broadcast_to(
                largest + jnp.log(totals), (QUERY_ROWS, HEAD_DIM)
            )


def attend(slots, seg_rows, seg_cols, qkv):
    blocks, rows, width = qkv.shape
    length = blocks * rows
    return pl.pallas_call(
        attend_kernel,
        out_shape=(
            jax.ShapeDtypeStruct((length, width // 3), BF16),
            jax.ShapeDtypeStruct((length, width // 3), F32),
        ),
        in_specs=[SMEM, VMEM, VMEM, VMEM],
        out_specs=(VMEM, VMEM),
        scratch_shapes=[pltpu.VMEM((length, width), BF16)],
        compiler_params=pltpu.CompilerParams(vmem_limit_bytes=48 * 1024 * 1024),
        name="attend",
    )(slots, seg_rows, seg_cols, qkv)


def attend_back_kernel(
    slot_ref, seg_row_ref, seg_col_ref, qkv_ref, log_ref, grad_ref, out_ref, held, total
):
    length = held.shape[0]
    width = grad_ref.shape[1]
    for block in range(length // 128):
        held[block * 128 : (block + 1) * 128, :] = qkv_ref[slot_ref[block]]
    for head in range(width // HEAD_DIM):
        at = slice(head * HEAD_DIM, (head + 1) * HEAD_DIM)
        key_at = slice(width + head * HEAD_DIM, width + (head + 1) * HEAD_DIM)
        value_at = slice(2 * width + head * HEAD_DIM, 2 * width + (head + 1) * HEAD_DIM)
        for first in reversed(range(0, length, QUERY_ROWS)):
            last = first + QUERY_ROWS
            query = held[first:last, at]
            key = held[:last, key_at]
            scores = masked_scores(
                query, key, first, seg_row_ref[first:last, :], seg_col_ref[:, :last]
            )
            probs = jnp.exp(scores - log_ref[first:last, head * HEAD_DIM : head * HEAD_DIM + 1])
            grad = grad_ref[first:last, at]
            grad_probs = lax.dot_general(
                grad, held[:last, value_at], (((1,), (1,)), ((), ())), preferred_element_type=F32
            )
            inner = jnp.sum(grad_probs * probs, axis=-1, keepdims=True)
            grad_scores = (probs * (grad_probs - inner) * SCORE_SCALE).astype(BF16)
            total[first:last, at] = jnp.dot(grad_scores, key, preferred_element_type=F32)
            grad_key = lax.dot_general(
                grad_scores, query, (((0,), (0,)), ((), ())), preferred_element_type=F32
            )
            grad_value = lax.dot_general(
                probs.astype(BF16), grad, (((0,), (0,)), ((), ())), preferred_element_type=F32
            )
            if last == length:
                total[:, key_at] = grad_key
                total[:, value_at] = grad_value
            else:
                total[:last, key_at] += grad_key
                total[:last, value_at] += grad_value
    for block in range(length // 128):
        out_ref[slot_ref[block]] = total[block * 128 : (block + 1) * 128, :]


def attend_back(slots, seg_rows, seg_cols, qkv, logs, grad):
    blocks, rows, width = qkv.shape
    length = blocks * rows
    return pl.pallas_call(
        attend_back_kernel,
        out_shape=jax.ShapeDtypeStruct(qkv.shape, F32),
        in_specs=[SMEM, VMEM, VMEM, VMEM, VMEM, VMEM],
        out_specs=VMEM,
        scratch_shapes=[pltpu.VMEM((length, width), BF16), pltpu.VMEM((length, width), F32)],
        compiler_params=pltpu.CompilerParams(vmem_limit_bytes=48 * 1024 * 1024),
        name="attend_back",
    )(slots, seg_rows, seg_cols, qkv, logs, grad)


def on_device(
    hidden_in,
    segment_ids,
    attention_gain,
    mlp_gain,
    query_base,
    query_left,
    query_right,
    query_magnitude,
    key_base,
    key_left,
    key_right,
    key_magnitude,
    value_base,
    value_left,
    value_right,
    value_magnitude,
    output_base,
    output_left,
    output_right,
    output_magnitude,
    gate_base,
    gate_left,
    gate_right,
    gate_magnitude,
    up_base,
    up_left,
    up_right,
    up_magnitude,
    down_base,
    down_left,
    down_right,
    down_magnitude,
    cotangent,
):
    z, xl = lax.axis_index("z"), lax.axis_index("xl")
    y, core = lax.axis_index("y"), lax.axis_index("core")
    resid = hidden_in[0].astype(F32)
    rows, width = resid.shape
    segments = segment_ids[0]
    length = segments.shape[0]
    blocks = length // rows
    heads_width = query_base.shape[1]
    hidden = gate_base.shape[1]

    normal_one, inverse_one, normed_one = rms_forward(resid, attention_gain)
    row_blocks = gather_row(normed_one)
    row_normed = jnp.concatenate(row_blocks, axis=0)
    slots = jnp.stack(
        [
            jnp.array(SLOT_AT, jnp.int32)[(block // 2 - z) % 4, (block % 2) ^ xl]
            for block in range(blocks)
        ]
    )
    block_of_slot = jnp.stack([2 * ((z + dz) % 4) + (xl ^ dx) for dz, dx in SLOTS])

    out_weight, out_squares = adapted_weight(output_base, output_left, output_right)
    query_weight, query_squares = adapted_weight(query_base, query_left, query_right)
    key_weight, key_squares = adapted_weight(key_base, key_left, key_right)
    value_weight, value_squares = adapted_weight(value_base, value_left, value_right)
    gate_weight, gate_squares = adapted_weight(gate_base, gate_left, gate_right)
    up_weight, up_squares = adapted_weight(up_base, up_left, up_right)
    down_weight, down_squares = adapted_weight(down_base, down_left, down_right)

    block_columns = width // 8
    piece = lax.dynamic_slice_in_dim(out_weight, (2 * y + core) * block_columns, block_columns, 1)
    column_own = of_everyone(piece, TENSOR).reshape(width, block_columns)
    y_up = lambda a: lax.ppermute(a, "y", UP)
    y_down = lambda a: lax.ppermute(a, "y", DOWN)
    half = width // 2
    column_below, column_above = y_up(column_own), y_down(column_own)
    column_far = jnp.concatenate([y_up(column_below[:half]), y_down(column_above[half:])], axis=0)
    relative = jnp.stack([column_own, column_above, column_far, column_below])
    ordered = jnp.stack([relative[(j - y) % 4] for j in range(4)])
    both = (ordered, core_swap(ordered))
    pair = [jnp.where(core == c, both[0], both[1]) for c in range(2)]
    whole_output = jnp.stack(pair, axis=1)
    whole_output = whole_output.transpose(2, 0, 1, 3).reshape(width, width)

    def other_half(weight):
        count = weight.shape[0] // 2
        pulled = from_x_neighbour(lax.dynamic_slice_in_dim(weight, core * count, count, 0))
        swapped = core_swap(pulled)
        return jnp.concatenate(
            [jnp.where(core == 0, pulled, swapped), jnp.where(core == 0, swapped, pulled)], axis=0
        )

    gate_other = other_half(gate_weight)
    up_other = other_half(up_weight)
    down_other = other_half(down_weight)

    gate_scale = gate_magnitude * lax.rsqrt(gate_squares)
    up_scale = up_magnitude * lax.rsqrt(up_squares)
    vectors = x_swap(jnp.stack([gate_scale, up_scale]))
    gate_scale_other, up_scale_other = vectors[0], vectors[1]
    factors = x_swap(
        jnp.concatenate([gate_right, up_right, down_left.T], axis=0).astype(BF16)
    )
    gate_right_other = factors[:RANK]
    up_right_other = factors[RANK : 2 * RANK]
    down_left_other = factors[2 * RANK :].T

    squares = of_everyone(jnp.stack([out_squares, down_squares]), TENSOR).sum(axis=0)
    out_norm, down_norm = jnp.sqrt(squares[0]), jnp.sqrt(squares[1])
    out_scale, down_scale = output_magnitude / out_norm, down_magnitude / down_norm
    whole_left = of_everyone(output_left.T.astype(BF16), TENSOR)
    whole_left = whole_left.transpose(1, 0, 2).reshape(RANK, width)

    cot_all = gather_z(cotangent[0])

    qkv_weight = jnp.concatenate([query_weight, key_weight, value_weight], axis=1)
    qkv_scale = jnp.concatenate([query_magnitude, key_magnitude, value_magnitude]) * lax.rsqrt(
        jnp.concatenate([query_squares, key_squares, value_squares])
    )
    qkv_values = dot(row_normed, qkv_weight) * qkv_scale
    index = jnp.arange(length, dtype=jnp.int32)
    change = jnp.concatenate([jnp.ones((1,), dtype=bool), segments[1:] != segments[:-1]])
    starts = lax.cummax(jnp.where(change, index, 0), axis=0)
    positions = (index - starts).astype(F32)
    positions = jnp.take(positions.reshape(blocks, rows), block_of_slot, axis=0).reshape(length)
    frequency = 10000.0 ** (-jnp.arange(0, HEAD_DIM, 2, dtype=F32) / HEAD_DIM)
    angles = positions[:, None] * frequency[None, :]
    cosine = jnp.concatenate([jnp.cos(angles), jnp.cos(angles)], axis=-1)[:, None, :]
    sine = jnp.concatenate([jnp.sin(angles), jnp.sin(angles)], axis=-1)[:, None, :]
    pairs = qkv_values[:, : 2 * heads_width].reshape(length, -1, HEAD_DIM)
    turned = (pairs * cosine + rotate_half(pairs) * sine).reshape(length, 2 * heads_width)
    qkv = jnp.concatenate([turned, qkv_values[:, 2 * heads_width :]], axis=1).astype(BF16)
    qkv = qkv.reshape(blocks, rows, 3 * heads_width)
    seg_rows, seg_cols = segments[:, None], segments[None, :]
    attended, logs = attend(slots, seg_rows, seg_cols, qkv)

    arrived = lax.all_to_all(attended, TENSOR, split_axis=0, concat_axis=1, tiled=True)
    out_raw = dot(arrived, whole_output)
    resid_two = resid + out_raw * out_scale
    normal_two, inverse_two, normed_two = rms_forward(resid_two, mlp_gain)
    normed_all = gather_z(normed_two)

    gate_value = dot(normed_all, gate_weight) * gate_scale
    up_value = dot(normed_all, up_weight) * up_scale
    gate_value_other = dot(normed_all, gate_other) * gate_scale_other
    up_value_other = dot(normed_all, up_other) * up_scale_other
    down_grad = (cot_all.astype(F32) * down_scale).astype(BF16)

    def activation(gate, upper, weight):
        sigmoid = jax.nn.sigmoid(gate)
        activated = (gate * sigmoid * upper).astype(BF16)
        grad_activated = dot_nt(down_grad, weight)
        grad_gate = grad_activated * upper * sigmoid * (1.0 + gate * (1.0 - sigmoid))
        grad_up = grad_activated * gate * sigmoid
        return activated, grad_gate, grad_up

    activated, grad_gate, grad_up = activation(gate_value, up_value, down_weight)
    activated_other, grad_gate_other, grad_up_other = activation(
        gate_value_other, up_value_other, down_other
    )
    gate_back = (grad_gate * gate_scale).astype(BF16)
    up_back = (grad_up * up_scale).astype(BF16)
    gate_back_other = (grad_gate_other * gate_scale_other).astype(BF16)
    up_back_other = (grad_up_other * up_scale_other).astype(BF16)
    grad_normed_all = (
        dot_nt(gate_back, gate_weight)
        + dot_nt(up_back, up_weight)
        + dot_nt(gate_back_other, gate_other)
        + dot_nt(up_back_other, up_other)
    ).astype(BF16)
    grad_normed_two = scatter_z(grad_normed_all, rows)
    grad_layer = cotangent[0].astype(F32)
    grad_resid_two = grad_layer + rms_backward(grad_normed_two, normal_two, inverse_two, mlp_gain)
    out_grad_raw = (grad_resid_two * out_scale).astype(BF16)
    head_part = dot_nt(out_grad_raw, whole_output).astype(BF16)
    grad_attended = lax.all_to_all(head_part, TENSOR, split_axis=1, concat_axis=0, tiled=True)

    down_raw = scatter_z(
        (dot(activated, down_weight) + dot(activated_other, down_other)).astype(BF16), rows
    )
    layer = resid_two + down_raw * down_scale

    gate_sum, up_sum = jnp.sum(grad_gate * gate_value, axis=0), jnp.sum(grad_up * up_value, axis=0)
    gate_sum_other = jnp.sum(grad_gate_other * gate_value_other, axis=0)
    up_sum_other = jnp.sum(grad_up_other * up_value_other, axis=0)
    low_gate_up = dot(normed_all, jnp.concatenate([gate_left, up_left], axis=1))
    low_gate, low_up = low_gate_up[:, :RANK], low_gate_up[:, RANK:]
    down_through = dot_nt(down_grad, down_right)
    sent = jnp.concatenate(
        [
            dot_tn(low_gate, gate_back_other),
            dot_tn(low_up, up_back_other),
            dot_tn(down_through, activated_other),
            gate_sum_other[None],
            up_sum_other[None],
        ],
        axis=0,
    )
    given = x_swap(sent.astype(BF16)).astype(F32)
    gate_sum = (gate_sum + given[3 * RANK]) / gate_magnitude
    up_sum = (up_sum + given[3 * RANK + 1]) / up_magnitude
    gate_right_part = dot_tn(low_gate, gate_back) + given[:RANK]
    up_right_part = dot_tn(low_up, up_back) + given[RANK : 2 * RANK]
    down_left_part = dot_tn(down_through, activated) + given[2 * RANK : 3 * RANK]

    def column_norm_terms(total, magnitude, weight, squares, left, right):
        coefficient = -total * magnitude / squares
        return (
            dot_nt(right * coefficient, weight),
            dot_tn(left, weight) * coefficient,
        )

    gate_left_norm, gate_right_norm = column_norm_terms(
        gate_sum, gate_magnitude, gate_weight, gate_squares, gate_left, gate_right
    )
    up_left_norm, up_right_norm = column_norm_terms(
        up_sum, up_magnitude, up_weight, up_squares, up_left, up_right
    )
    gate_through = dot_nt(gate_back, gate_right) + dot_nt(gate_back_other, gate_right_other)
    up_through = dot_nt(up_back, up_right) + dot_nt(up_back_other, up_right_other)
    throughs = jnp.concatenate([gate_through, up_through], axis=1)
    gate_up_left = dot_tn(throughs, normed_all)
    gate_left_part = FACTOR * (gate_up_left[:RANK] + gate_left_norm)
    up_left_part = FACTOR * (gate_up_left[RANK:] + up_left_norm)
    gate_right_part = FACTOR * (gate_right_part + gate_right_norm)
    up_right_part = FACTOR * (up_right_part + up_right_norm)

    low_down = dot(activated, down_left) + dot(activated_other, down_left_other)
    out_low = dot_nt(arrived, whole_left)
    out_through = dot_nt(out_grad_raw, output_right)
    out_sum_part = jnp.sum(grad_resid_two * out_raw, axis=0)
    down_sum_part = jnp.sum(grad_layer * down_raw, axis=0)
    row_sums = of_everyone(jnp.stack([out_sum_part, down_sum_part]), TENSOR).sum(axis=0)
    out_coefficient = -row_sums[0] * output_magnitude / (out_norm * out_norm * out_norm)
    down_coefficient = -row_sums[1] * down_magnitude / (down_norm * down_norm * down_norm)
    out_right_part = FACTOR * (
        dot_tn(out_low, out_grad_raw) + dot_tn(output_left, out_weight) * out_coefficient
    )
    down_right_part = FACTOR * (
        dot_tn(low_down, down_grad) + dot_tn(down_left, down_weight) * down_coefficient
    )
    through_row = of_everyone(out_through.T.astype(BF16), TENSOR)
    through_row = through_row.transpose(1, 0, 2).reshape(RANK, length)
    out_left_part = FACTOR * (
        dot(through_row, attended) + dot_nt(output_right * out_coefficient, out_weight)
    )
    down_left_part = FACTOR * (
        down_left_part + dot_nt(down_right * down_coefficient, down_weight)
    )
    middle = summed(
        [gate_left_part, up_left_part, out_right_part, down_right_part, out_sum_part, down_sum_part],
        ALL,
    )
    middle_split = summed(
        [gate_right_part, up_right_part, out_left_part, down_left_part, gate_sum, up_sum], DP
    )

    grad_qkv = attend_back(slots, seg_rows, seg_cols, qkv, logs, grad_attended)
    grad_qkv = grad_qkv.reshape(length, 3 * heads_width)
    grad_pairs = grad_qkv[:, : 2 * heads_width].reshape(length, -1, HEAD_DIM)
    grad_pairs = (grad_pairs * cosine - rotate_half(grad_pairs * sine)).reshape(
        length, 2 * heads_width
    )
    grad_qkv = jnp.concatenate([grad_pairs, grad_qkv[:, 2 * heads_width :]], axis=1)
    qkv_back = (grad_qkv * qkv_scale).astype(BF16)
    grad_row = dot_nt(qkv_back, qkv_weight).astype(BF16)
    grad_normed_one = scatter_row([grad_row[s * rows : (s + 1) * rows] for s in range(blocks)])
    input_grad = grad_resid_two + rms_backward(
        grad_normed_one, normal_one, inverse_one, attention_gain
    )
    qkv_magnitude = jnp.concatenate([query_magnitude, key_magnitude, value_magnitude])
    qkv_sum = jnp.sum(grad_qkv * qkv_values, axis=0) / qkv_magnitude
    lefts = jnp.concatenate([query_left, key_left, value_left], axis=1)
    lows = dot(row_normed, lefts)
    last, last_split = [], []
    throughs, norms = [], []
    for i, (weight, squares_of, left, right, magnitude) in enumerate(
        (
            (query_weight, query_squares, query_left, query_right, query_magnitude),
            (key_weight, key_squares, key_left, key_right, key_magnitude),
            (value_weight, value_squares, value_left, value_right, value_magnitude),
        )
    ):
        at = slice(i * heads_width, (i + 1) * heads_width)
        back = qkv_back[:, at]
        left_norm, right_norm = column_norm_terms(
            qkv_sum[at], magnitude, weight, squares_of, left, right
        )
        throughs.append(dot_nt(back, right))
        norms.append(left_norm)
        last_split.append(
            FACTOR * (dot_tn(lows[:, i * RANK : (i + 1) * RANK], back) + right_norm)
        )
    left_parts = dot_tn(jnp.concatenate(throughs, axis=1), row_normed)
    last = FACTOR * (left_parts + jnp.concatenate(norms, axis=0))
    (last,) = summed([last], ALL)
    last_split = summed(last_split + [qkv_sum], DP)
    qkv_magnitude_grad = last_split[3]
    return (
        layer.astype(BF16)[None],
        input_grad[None],
        last[:RANK].T,
        last_split[0],
        qkv_magnitude_grad[:heads_width],
        last[RANK : 2 * RANK].T,
        last_split[1],
        qkv_magnitude_grad[heads_width : 2 * heads_width],
        last[2 * RANK :].T,
        last_split[2],
        qkv_magnitude_grad[2 * heads_width :],
        middle_split[2].T,
        middle[2],
        middle[4] / out_norm,
        middle[0].T,
        middle_split[0],
        middle_split[4],
        middle[1].T,
        middle_split[1],
        middle_split[5],
        middle_split[3].T,
        middle[3],
        middle[5] / down_norm,
    )


def solution(mesh):
    torus = Mesh(mesh.devices.reshape(4, 2, 2, 4, 2), ("y", "xh", "core", "z", "xl"))
    column = (P(None, TENSOR), P(), P(None, TENSOR), P(TENSOR))
    row = (P(TENSOR, None), P(TENSOR, None), P(), P())
    column_out, row_out = column[1:], row[1:]
    tokens = P(DP, TENSOR, None)
    return jax.shard_map(
        on_device,
        mesh=torus,
        in_specs=(
            tokens,
            P(DP, None),
            P(),
            P(),
            *column,
            *column,
            *column,
            *row,
            *column,
            *column,
            *row,
            tokens,
        ),
        out_specs=(
            tokens,
            tokens,
            *column_out,
            *column_out,
            *column_out,
            *row_out,
            *column_out,
            *column_out,
            *row_out,
        ),
        check_vma=False,
    )
```

time: 1180 us -> 559 us (0.47)
  waiting for transfers between devices: 462 us -> 95.8 us
  matrix products: 369 us -> 113 us
  blocking collectives: 64.4 us -> 0 us
  starting transfers between devices: 105 us -> 145 us
  local copies, waits for them, and re-layouts: 65.3 us -> 95.6 us
  Pallas kernels: 0 us -> 14.2 us
  between operations: 15.8 us -> 3.72 us
    dot_general x91 -> x63, matrix products: 369 us -> 113 us  [the longest x19 47.9 us: dot(): jnp.dot(left.astype(BF16), right.astype(BF16), preferred_element_type=F32)]
    all_gather x5 -> x0, waiting for transfers between devices: 243 us -> none  [the longest x1 77.9 us: on_device(): gathered_two = lax.all_gather(normed_two, TENSOR, axis=0, tiled=True)]
    reduce_scatter x3 -> x0, waiting for transfers between devices: 145 us -> none  [the longest x1 91.8 us: on_device(): lax.psum_scatter((plain_dot(rows_of(activated, first_row, local_rows * la...]
    ppermute x0 -> x44, starting transfers between devices: none -> 65.9 us  [the longest x14 30.7 us: z_down(): return lax.ppermute(array, 'z', DOWN)]
    psum x1 -> x0, blocking collectives: 64.4 us -> none  [on_device(): lax.psum((query_back[2], key_back[2], value_back[2], gate_back[2], up_bac...]
    ppermute x0 -> x44, waiting for transfers between devices: none -> 35.7 us  [the longest x14 16.8 us: z_up(): return lax.ppermute(array, 'z', UP)]
    all_to_all x20 -> x15, starting transfers between devices: 104 us -> 79.2 us  [the longest x13 71.9 us: all_to_all(): return lax.all_to_all(array, axes, 0, 0, tiled=True)]
    another operation x2 -> x11, other arithmetic: 0.31 us -> 19.2 us  [the longest x2 13.3 us: on_device(): whole_output = jnp.stack(pair, axis=1)]
  transfers between devices with their start and end apart: 29 -> 59, of which waited for: 21 -> 21; matrix products, arithmetic and copies ran while one was open for 26% -> 43% of each run, Pallas kernels for 0% -> 1%
where the time goes in v1:
time: 559 us; the launch traced here: 551 us
  starting transfers between devices  145 us (26%)
  matrix products  113 us (20%)
  waiting for transfers between devices  95.8 us (17%)
  local copies, waits for them, and re-layouts  95.6 us (17%)
  other arithmetic  82.8 us (15%)
  Pallas kernels  14.2 us (3%)
    all_to_all x13, starting transfers between devices, all_to_all(): return lax.all_to_all(array, axes, 0, 0, tiled=True)  71.9 us
    all_to_all x13, waiting for transfers between devices, all_to_all(): return lax.all_to_all(array, axes, 0, 0, tiled=True)  53.1 us
    dot_general x19, matrix products, dot(): jnp.dot(left.astype(BF16), right.astype(BF16), preferred_element_type=F32)  47.9 us
    dot_general x24, matrix products, dot_nt(): lax.dot_general(left.astype(BF16), right.astype(BF16), (((1,), (1,)), (()...  46.2 us
    unnamed x393, local copies, waits for them, and re-layouts  32 us
    ppermute x14, starting transfers between devices, z_down(): return lax.ppermute(array, 'z', DOWN)  30.7 us
    dot_general x20, matrix products, dot_tn(): lax.dot_general(left.astype(BF16), right.astype(BF16), (((0,), (0,)), (()...  19.2 us
    ppermute x14, waiting for transfers between devices, z_up(): return lax.ppermute(array, 'z', UP)  16.8 us
  transfers between devices with their start and end apart: 59, of which 21 were waited for; matrix products, arithmetic and copies ran while one was open for 43% of the time, Pallas kernels for 1%

profile of v1, /device:TPU:1, one launch (start us, length us, event | category | flops | bytes accessed | tf_op | source)
XLA Modules:
  0.0 550.7 jit_solution(9793988046349651439)
XLA Ops:
  25.1 4.2 all-to-all-start.2
  61.5 5.1 stack.95.slot_ref
  71.4 4.2 all-to-all-start.1
  85.9 5.9 %all-to-all-done.1 = bf16[8,256,256]{1,2,0:T(8,128)(2,1)} async-done(((bf16[8,256,256]{1,2,0:T(8,128)(2,1)}), bf16[8,256,256]{1,2,0:T(8,128)(2,1)}, u32[]{:S(2)}, u32[]{:S(2)}) %all-to-all-start.1) | async-done | bytes 1048608 | tf_op jit(solution)/shard_map/all_to_all | solution.py:101
  108.2 5.2 collective-permute-done.8
  136.8 9.2 %collective-permute-start.11 = (bf16[4,2048,256]{1,2,0:T(8,128)(2,1)}, bf16[4,2048,256]{1,2,0:T(8,128)(2,1)}, u32[]{:S(2)}, u32[]{:S(2)}) collective-permute-start(bf16[4,2048,256]{1,2,0:T(8,128)(2,1)} %pad_maximum_fusion.2), channel_id=1, source_target_pairs={{0,8},{8,0},{1,9},{9,1},{2,10},{10,2},{3,11},{11,3},{4,12},{12,4},... | collective-permute-start | bytes 12582920 | tf_op jit(solution)/shard_map/ppermute | solution.py:41
  148.9 4.4 collective-permute-start.20
  166.9 5.9 %attend.1 = (bf16[1024,256]{1,0:T(8,128)(2,1)}, f32[1024,256]{1,0:T(8,128)S(1)}) custom-call(s32[8]{0:T(128)S(1)} %stack.95.slot_ref, s32[1024,1]{1,0:T(8,128)S(1)} %copy.89.seg_row_ref, s32[1,1024]{1,0:T(1,128)S(1)} %copy-done.2, bf16[8,128,768]{2,1,0:T(8,128)(2,1)S(1)} %pad_maximum_fusion.17.qkv_ref), custom_call_target="tpu_custom_call" | custom-call | tf_op jit(solution)/shard_map/attend/pallas_call | solution.py:210
  199.3 5.7 %select_bitcast_fusion.1 = (bf16[4,1,2048,256]{2,3,1,0:T(8,128)(2,1)}, bf16[4,1,2048,256]{2,3,1,0:T(8,128)(2,1)}) fusion(bf16[4,2048,256]{1,2,0:T(8,128)(2,1)} %collective-permute-done.11, pred[]{:T(512)S(6)} %eq.33, bf16[1,2048,256]{1,2,0:T(8,128)(2,1)S(1)} %copy-done.29, bf16[1,2048,256]{1,2,0:T(8,128)(2,1)S(1)} %copy-done.31, ...), kind=kLoop, calls=%fused_computation.14 | loop fusion | flops 10485760 | bytes 16777218 | tf_op jit(solution)/shard_map/stack | solution.py:356
  205.0 7.7 %pad_maximum_fusion = bf16[4,2,2048,256]{2,3,1,0:T(8,128)(2,1)} fusion(bf16[4,1,2048,256]{2,3,1,0:T(8,128)(2,1)} %get-tuple-element.46, bf16[4,1,2048,256]{2,3,1,0:T(8,128)(2,1)} %get-tuple-element.45), kind=kLoop, calls=%fused_computation.1 | loop fusion | flops 4194304 | bytes 16777216 | tf_op jit(solution)/shard_map/stack | solution.py:356
  212.7 7.3 %multiply_reduce_fusion.14 = (f32[128]{0:T(128)S(1)}, f32[128,2048]{1,0:T(8,128)S(1)}, f32[128,2048]{1,0:T(8,128)}) fusion(f32[2048]{0:T(1024)S(1)} %copy-done.117, bf16[1,128,2048]{2,1,0:T(8,128)(2,1)S(1)} %copy-done.21, bf16[128,2048]{0,1:T(8,128)(2,1)S(1)} %bitcast.308, bf16[2048,2048]{0,1:T(8,128)(2,1)} %bitcast.295), kind=kOutput, calls=%fused_computation.170 | convolution fusion | flops 1075052416 | bytes 11543040 | tf_op jit(solution)/shard_map/dot_general | solution.py:126
  226.7 5.5 %collective-permute-done.13 = bf16[128,2048]{1,0:T(8,128)(2,1)S(1)} collective-permute-done((bf16[128,2048]{1,0:T(8,128)(2,1)S(1)}, bf16[128,2048]{1,0:T(8,128)(2,1)S(1)}, u32[]{:S(2)}, u32[]{:S(2)}) %collective-permute-start.13) | collective-permute-done | bytes 524320 | tf_op jit(solution)/shard_map/ppermute | solution.py:33
  236.1 6.3 %collective-permute-done.14 = bf16[64,2048]{1,0:T(8,128)(2,1)S(1)} collective-permute-done((bf16[64,2048]{1,0:T(8,128)(2,1)S(1)}, bf16[64,2048]{1,0:T(8,128)(2,1)S(1)}, u32[]{:S(2)}, u32[]{:S(2)}) %collective-permute-start.14) | collective-permute-done | bytes 262176 | tf_op jit(solution)/shard_map/ppermute | solution.py:29
  257.8 4.3 fusion.192
  273.5 7.9 %add_convert_fusion = bf16[512,2048]{1,0:T(8,128)(2,1)S(1)} fusion(f32[512,2048]{1,0:T(8,128)} %fusion.17, f32[512,2048]{1,0:T(8,128)} %fusion.192, f32[512,2048]{1,0:T(8,128)} %fusion.193, bf16[512,704]{0,1:T(8,128)(2,1)} %copy-done.37, bf16[1024,704]{0,1:T(8,128)(2,1)} %get-tuple-element.78, bf16[1024,704]{0,1:T(8,128)(2,1)} %get-tuple-element.77), kind=kOutput, calls=%fused_computation.10 | convolution fusion | flops 1486356480 | bytes 18284544 | tf_op jit(solution)/shard_map/dot_general | solution.py:130
  309.7 6.8 %collective-permute-done.26 = bf16[128,2048]{1,0:T(8,128)(2,1)} collective-permute-done((bf16[128,2048]{1,0:T(8,128)(2,1)}, bf16[128,2048]{1,0:T(8,128)(2,1)}, u32[]{:S(2)}, u32[]{:S(2)}) %collective-permute-start.26) | collective-permute-done | bytes 524320 | tf_op jit(solution)/shard_map/ppermute | solution.py:33
  356.0 14.7 %all-to-all-start.10 = ((bf16[16,20,128]{2,1,0:T(8,128)(2,1)}), bf16[16,20,128]{2,1,0:T(8,128)(2,1)S(1)}, u32[]{:S(2)}, u32[]{:S(2)}) async-start(bf16[16,20,128]{2,1,0:T(8,128)(2,1)} %reshape.694), calls=%async_computation.10 | async-start | bytes 196608 | tf_op jit(solution)/shard_map/all_to_all | solution.py:101
  372.6 5.5 %all-to-all-done.10 = bf16[16,20,128]{2,1,0:T(8,128)(2,1)S(1)} async-done(((bf16[16,20,128]{2,1,0:T(8,128)(2,1)}), bf16[16,20,128]{2,1,0:T(8,128)(2,1)S(1)}, u32[]{:S(2)}, u32[]{:S(2)}) %all-to-all-start.10) | async-done | bytes 81952 | tf_op jit(solution)/shard_map/all_to_all | solution.py:101
  385.2 4.9 all-to-all-done.11
  394.1 4.7 convolution_convert_fusion.1
  399.6 8.4 %all-to-all-done.13 = bf16[128,9,128]{2,1,0:T(8,128)(2,1)S(1)} async-done(((bf16[128,9,128]{2,1,0:T(8,128)(2,1)}), bf16[128,9,128]{2,1,0:T(8,128)(2,1)S(1)}, u32[]{:S(2)}, u32[]{:S(2)}) %all-to-all-start.13) | async-done | bytes 294944 | tf_op jit(solution)/shard_map/all_to_all | solution.py:101
  415.3 5.4 all-to-all-done.3
  421.9 8.3 %attend_back.1 = f32[8,128,768]{2,1,0:T(8,128)} custom-call(s32[8]{0:T(128)S(1)} %stack.95.slot_ref, s32[1024,1]{1,0:T(8,128)S(1)} %copy.89.seg_row_ref, s32[1,1024]{1,0:T(1,128)S(1)} %copy-done.2, bf16[8,128,768]{2,1,0:T(8,128)(2,1)S(1)} %pad_maximum_fusion.17.qkv_ref, f32[1024,256]{1,0:T(8,128)S(1)} %copy-done.1, bf16[1024,256]{1,0:T(8,128)(2,1)S(1)} %bitcast.293), custom_call_target="tpu_custom_call" | custom-call | tf_op jit(solution)/shard_map/attend_back/pallas_call | solution.py:269
  446.6 5.3 convolution_convert_fusion
  454.7 5.3 all-to-all-start.6
  468.0 6.3 %all-to-all-start.7 = ((bf16[16,7,128]{2,1,0:T(8,128)(2,1)}), bf16[16,7,128]{2,1,0:T(8,128)(2,1)S(1)}, u32[]{:S(2)}, u32[]{:S(2)}) async-start(bf16[16,7,128]{2,1,0:T(8,128)(2,1)} %broadcast_in_dim.56), calls=%async_computation.7 | async-start | bytes 65536 | tf_op jit(solution)/shard_map/all_to_all | solution.py:101
  481.6 6.8 %all-to-all-start.4 = ((bf16[128,6,128]{2,1,0:T(8,128)(2,1)}), bf16[128,6,128]{2,1,0:T(8,128)(2,1)S(1)}, u32[]{:S(2)}, u32[]{:S(2)}) async-start(bf16[128,6,128]{2,1,0:T(8,128)(2,1)} %reshape.684), calls=%async_computation.4 | async-start | bytes 524288 | tf_op jit(solution)/shard_map/all_to_all | solution.py:101
  489.0 10.4 %all-to-all-done.4 = bf16[128,6,128]{2,1,0:T(8,128)(2,1)S(1)} async-done(((bf16[128,6,128]{2,1,0:T(8,128)(2,1)}), bf16[128,6,128]{2,1,0:T(8,128)(2,1)S(1)}, u32[]{:S(2)}, u32[]{:S(2)}) %all-to-all-start.4) | async-done | bytes 196640 | tf_op jit(solution)/shard_map/all_to_all | solution.py:101
  500.3 6.3 %all-to-all-start.14 = ((bf16[128,9,128]{2,1,0:T(8,128)(2,1)}), bf16[128,9,128]{2,1,0:T(8,128)(2,1)S(1)}, u32[]{:S(2)}, u32[]{:S(2)}) async-start(bf16[128,9,128]{2,1,0:T(8,128)(2,1)} %broadcast_in_dim.63), calls=%async_computation.14 | async-start | bytes 1048576 | tf_op jit(solution)/shard_map/all_to_all | solution.py:101
  513.2 7.1 %all-to-all-done.14 = bf16[128,9,128]{2,1,0:T(8,128)(2,1)S(1)} async-done(((bf16[128,9,128]{2,1,0:T(8,128)(2,1)}), bf16[128,9,128]{2,1,0:T(8,128)(2,1)S(1)}, u32[]{:S(2)}, u32[]{:S(2)}) %all-to-all-start.14) | async-done | bytes 294944 | tf_op jit(solution)/shard_map/all_to_all | solution.py:101
  521.1 5.5 all-to-all-start.5
  539.3 6.7 %collective-permute-done.36 = bf16[128,2048]{1,0:T(8,128)(2,1)S(1)} collective-permute-done((bf16[128,2048]{1,0:T(8,128)(2,1)}, bf16[128,2048]{1,0:T(8,128)(2,1)S(1)}, u32[]{:S(2)}, u32[]{:S(2)}) %collective-permute-start.36) | collective-permute-done | bytes 524320 | tf_op jit(solution)/shard_map/ppermute | solution.py:29
  (715 shorter events, 339.7 us)
Async XLA Ops:
  0.7 80.0 %collective-permute-start.27 = (bf16[128,2048]{1,0:T(8,128)(2,1)}, bf16[128,2048]{1,0:T(8,128)(2,1)}, u32[]{:S(2)}, u32[]{:S(2)}) collective-permute-start(bf16[128,2048]{1,0:T(8,128)(2,1)} %bitcast.312), channel_id=1, source_target_pairs={{0,2},{2,4},{4,6},{6,0},{1,3},{3,5},{5,7},{7,1},{8,10},{10,12},{12... | collective-permute-start | bytes 1572872 | tf_op jit(solution)/shard_map/ppermute | solution.py:29
  3.2 80.7 %collective-permute-start.28 = (bf16[128,2048]{1,0:T(8,128)(2,1)}, bf16[128,2048]{1,0:T(8,128)(2,1)}, u32[]{:S(2)}, u32[]{:S(2)}) collective-permute-start(bf16[128,2048]{1,0:T(8,128)(2,1)} %bitcast.313), channel_id=1, source_target_pairs={{0,6},{2,0},{4,2},{6,4},{1,7},{3,1},{5,3},{7,5},{8,14},{10,8},{12,... | collective-permute-start | bytes 1572872 | tf_op jit(solution)/shard_map/ppermute | solution.py:33
  9.6 92.4 %collective-permute-start.2 = (bf16[128,2048]{1,0:T(8,128)(2,1)}, bf16[128,2048]{1,0:T(8,128)(2,1)}, u32[]{:S(2)}, u32[]{:S(2)}) collective-permute-start(bf16[128,2048]{1,0:T(8,128)(2,1)} %get-tuple-element.44), channel_id=1, source_target_pairs={{0,6},{2,0},{4,2},{6,4},{1,7},{3,1},{5,3},{7,5},{8,14},{10,8},{12,... | collective-permute-start | bytes 1572872 | tf_op jit(solution)/shard_map/ppermute | solution.py:33
  11.0 88.0 %collective-permute-start.1 = (bf16[128,2048]{1,0:T(8,128)(2,1)}, bf16[128,2048]{1,0:T(8,128)(2,1)}, u32[]{:S(2)}, u32[]{:S(2)}) collective-permute-start(bf16[128,2048]{1,0:T(8,128)(2,1)} %get-tuple-element.44), channel_id=1, source_target_pairs={{0,2},{2,4},{4,6},{6,0},{1,3},{3,5},{5,7},{7,1},{8,10},{10,12},{12... | collective-permute-start | bytes 1572872 | tf_op jit(solution)/shard_map/ppermute | solution.py:29
  18.7 47.9 %collective-permute-start.18 = (f32[2,704]{1,0:T(2,128)}, f32[2,704]{1,0:T(2,128)}, u32[]{:S(2)}, u32[]{:S(2)}) collective-permute-start(f32[2,704]{1,0:T(2,128)} %pad_maximum_fusion.33), channel_id=1, source_target_pairs={{0,1},{1,0},{2,3},{3,2},{4,5},{5,4},{6,7},{7,6},{8,9},{9,8},{10,11... | collective-permute-start | bytes 16904 | tf_op jit(solution)/shard_map/ppermute | solution.py:37
  25.1 44.4 %all-to-all-start.2 = ((f32[8,2,2048]{2,1,0:T(2,128)}), f32[8,2,2048]{2,1,0:T(2,128)}, u32[]{:S(2)}, u32[]{:S(2)}) async-start(f32[8,2,2048]{2,1,0:T(2,128)} %broadcast_in_dim.50), calls=%async_computation.2 | async-start | bytes 262144 | tf_op jit(solution)/shard_map/all_to_all | solution.py:101
  66.6 27.9 %collective-permute-start = (bf16[128,2048]{1,0:T(8,128)(2,1)}, bf16[128,2048]{1,0:T(8,128)(2,1)}, u32[]{:S(2)}, u32[]{:S(2)}) collective-permute-start(bf16[128,2048]{1,0:T(8,128)(2,1)} %get-tuple-element.44), channel_id=1, source_target_pairs={{0,1},{1,0},{2,3},{3,2},{4,5},{5,4},{6,7},{7,6},{8,9},{9,8},{10,11... | collective-permute-start | bytes 1572872 | tf_op jit(solution)/shard_map/ppermute | solution.py:37
  71.4 20.3 %all-to-all-start.1 = ((bf16[8,256,256]{1,2,0:T(8,128)(2,1)}), bf16[8,256,256]{1,2,0:T(8,128)(2,1)}, u32[]{:S(2)}, u32[]{:S(2)}) async-start(bf16[8,256,256]{1,2,0:T(8,128)(2,1)} %broadcast_in_dim.49), calls=%async_computation.1 | async-start | bytes 2097152 | tf_op jit(solution)/shard_map/all_to_all | solution.py:101
  80.7 67.8 %collective-permute-start.19 = (bf16[1024,704]{0,1:T(8,128)(2,1)}, bf16[1024,704]{0,1:T(8,128)(2,1)}, u32[]{:S(2)}, u32[]{:S(2)}) collective-permute-start(bf16[1024,704]{0,1:T(8,128)(2,1)} %constant_dynamic-slice_fusion.1), channel_id=1, source_target_pairs={{17,0},{9,8},{16,1},{8,9},{1,16},{25,24},{0,17},{24,25},{19,2},{11... | collective-permute-start | bytes 4325384 | tf_op jit(solution)/shard_map/ppermute | solution.py:52
  93.1 20.3 %collective-permute-start.8 = (bf16[2048,256]{0,1:T(8,128)(2,1)S(1)}, bf16[2048,256]{0,1:T(8,128)(2,1)S(1)}, u32[]{:S(2)}, u32[]{:S(2)}) collective-permute-start(bf16[2048,256]{0,1:T(8,128)(2,1)S(1)} %bitcast.314), channel_id=1, source_target_pairs={{0,32},{32,64},{64,96},{96,0},{1,33},{33,65},{65,97},{97,1},{2,34}... | collective-permute-start | bytes 3145736 | tf_op jit(solution)/shard_map/ppermute | solution.py:347
  94.5 20.8 %collective-permute-start.7 = (bf16[2048,256]{0,1:T(8,128)(2,1)S(1)}, bf16[2048,256]{0,1:T(8,128)(2,1)S(1)}, u32[]{:S(2)}, u32[]{:S(2)}) collective-permute-start(bf16[2048,256]{0,1:T(8,128)(2,1)S(1)} %bitcast.315), channel_id=1, source_target_pairs={{0,96},{32,0},{64,32},{96,64},{1,97},{33,1},{65,33},{97,65},{2,98}... | collective-permute-start | bytes 3145736 | tf_op jit(solution)/shard_map/ppermute | solution.py:348
  106.6 20.9 %collective-permute-start.4 = (bf16[128,2048]{1,0:T(8,128)(2,1)}, bf16[128,2048]{1,0:T(8,128)(2,1)}, u32[]{:S(2)}, u32[]{:S(2)}) collective-permute-start(bf16[128,2048]{1,0:T(8,128)(2,1)} %collective-permute-done), channel_id=1, source_target_pairs={{0,6},{2,0},{4,2},{6,4},{1,7},{3,1},{5,3},{7,5},{8,14},{10,8},{12,... | collective-permute-start | bytes 1572872 | tf_op jit(solution)/shard_map/ppermute | solution.py:33
  125.4 23.5 %collective-permute-start.21 = (bf16[352,2048]{1,0:T(8,128)(2,1)}, bf16[352,2048]{1,0:T(8,128)(2,1)}, u32[]{:S(2)}, u32[]{:S(2)}) collective-permute-start(bf16[352,2048]{1,0:T(8,128)(2,1)} %constant_dynamic-slice_fusion), channel_id=1, source_target_pairs={{17,0},{9,8},{16,1},{8,9},{1,16},{25,24},{0,17},{24,25},{19,2},{11... | collective-permute-start | bytes 4325384 | tf_op jit(solution)/shard_map/ppermute | solution.py:52
  127.5 19.6 %collective-permute-start.5 = (bf16[128,2048]{1,0:T(8,128)(2,1)}, bf16[128,2048]{1,0:T(8,128)(2,1)S(1)}, u32[]{:S(2)}, u32[]{:S(2)}) collective-permute-start(bf16[128,2048]{1,0:T(8,128)(2,1)} %collective-permute-done.1), channel_id=1, source_target_pairs={{0,2},{2,4},{4,6},{6,0},{1,3},{3,5},{5,7},{7,1},{8,10},{10,12},{12... | collective-permute-start | bytes 1572872 | tf_op jit(solution)/shard_map/ppermute | solution.py:29
  127.5 25.8 %collective-permute-start.6 = (bf16[128,2048]{1,0:T(8,128)(2,1)}, bf16[128,2048]{1,0:T(8,128)(2,1)S(1)}, u32[]{:S(2)}, u32[]{:S(2)}) collective-permute-start(bf16[128,2048]{1,0:T(8,128)(2,1)} %collective-permute-done.4), channel_id=1, source_target_pairs={{0,6},{2,0},{4,2},{6,4},{1,7},{3,1},{5,3},{7,5},{8,14},{10,8},{12,... | collective-permute-start | bytes 1572872 | tf_op jit(solution)/shard_map/ppermute | solution.py:33
  136.8 62.5 %collective-permute-start.11 = (bf16[4,2048,256]{1,2,0:T(8,128)(2,1)}, bf16[4,2048,256]{1,2,0:T(8,128)(2,1)}, u32[]{:S(2)}, u32[]{:S(2)}) collective-permute-start(bf16[4,2048,256]{1,2,0:T(8,128)(2,1)} %pad_maximum_fusion.2), channel_id=1, source_target_pairs={{0,8},{8,0},{1,9},{9,1},{2,10},{10,2},{3,11},{11,3},{4,12},{12,4},... | collective-permute-start | bytes 12582920 | tf_op jit(solution)/shard_map/ppermute | solution.py:41
  147.2 139.4 %collective-permute-start.43 = (bf16[48,704]{1,0:T(8,128)(2,1)}, bf16[48,704]{1,0:T(8,128)(2,1)}, u32[]{:S(2)}, u32[]{:S(2)}) collective-permute-start(bf16[48,704]{1,0:T(8,128)(2,1)} %pad_maximum_fusion.30), channel_id=1, source_target_pairs={{0,1},{1,0},{2,3},{3,2},{4,5},{5,4},{6,7},{7,6},{8,9},{9,8},{10,11... | collective-permute-start | bytes 202760 | tf_op jit(solution)/shard_map/ppermute | solution.py:37
  148.5 31.8 %collective-permute-start.16 = (bf16[1024,704]{0,1:T(8,128)(2,1)}, bf16[1024,704]{0,1:T(8,128)(2,1)}, u32[]{:S(2)}, u32[]{:S(2)}) collective-permute-start(bf16[1024,704]{0,1:T(8,128)(2,1)} %constant_dynamic-slice_fusion.2), channel_id=1, source_target_pairs={{17,0},{9,8},{16,1},{8,9},{1,16},{25,24},{0,17},{24,25},{19,2},{11... | collective-permute-start | bytes 4325384 | tf_op jit(solution)/shard_map/ppermute | solution.py:52
  148.9 43.6 %collective-permute-start.20 = (bf16[1024,704]{0,1:T(8,128)(2,1)}, bf16[1024,704]{0,1:T(8,128)(2,1)}, u32[]{:S(2)}, u32[]{:S(2)}) collective-permute-start(bf16[1024,704]{0,1:T(8,128)(2,1)} %collective-permute-done.19), channel_id=1, source_target_pairs={{0,8},{8,0},{1,9},{9,1},{2,10},{10,2},{3,11},{11,3},{4,12},{12,4},... | collective-permute-start | bytes 4325384 | tf_op jit(solution)/shard_map/ppermute | solution.py:41
  153.3 42.8 %collective-permute-start.22 = (bf16[352,2048]{1,0:T(8,128)(2,1)}, bf16[352,2048]{1,0:T(8,128)(2,1)}, u32[]{:S(2)}, u32[]{:S(2)}) collective-permute-start(bf16[352,2048]{1,0:T(8,128)(2,1)} %collective-permute-done.21), channel_id=1, source_target_pairs={{0,8},{8,0},{1,9},{9,1},{2,10},{10,2},{3,11},{11,3},{4,12},{12,4},... | collective-permute-start | bytes 4325384 | tf_op jit(solution)/shard_map/ppermute | solution.py:41
  180.3 42.6 %collective-permute-start.17 = (bf16[1024,704]{0,1:T(8,128)(2,1)}, bf16[1024,704]{0,1:T(8,128)(2,1)}, u32[]{:S(2)}, u32[]{:S(2)}) collective-permute-start(bf16[1024,704]{0,1:T(8,128)(2,1)} %collective-permute-done.16), channel_id=1, source_target_pairs={{0,8},{8,0},{1,9},{9,1},{2,10},{10,2},{3,11},{11,3},{4,12},{12,4},... | collective-permute-start | bytes 4325384 | tf_op jit(solution)/shard_map/ppermute | solution.py:41
  187.4 136.5 %all-to-all-start.12 = ((bf16[8,16,256]{2,1,0:T(8,128)(2,1)}), bf16[8,16,256]{2,1,0:T(8,128)(2,1)}, u32[]{:S(2)}, u32[]{:S(2)}) async-start(bf16[8,16,256]{2,1,0:T(8,128)(2,1)} %broadcast_in_dim.62), calls=%async_computation.12 | async-start | bytes 131072 | tf_op jit(solution)/shard_map/all_to_all | solution.py:101
  272.3 19.5 %collective-permute-start.42 = (bf16[50,704]{1,0:T(8,128)(2,1)S(1)}, bf16[50,704]{1,0:T(8,128)(2,1)S(1)}, u32[]{:S(2)}, u32[]{:S(2)}) collective-permute-start(bf16[50,704]{1,0:T(8,128)(2,1)S(1)} %concatenate.169), channel_id=1, source_target_pairs={{0,1},{1,0},{2,3},{3,2},{4,5},{5,4},{6,7},{7,6},{8,9},{9,8},{10,11... | collective-permute-start | bytes 211208 | tf_op jit(solution)/shard_map/ppermute | solution.py:37
  356.0 22.1 %all-to-all-start.10 = ((bf16[16,20,128]{2,1,0:T(8,128)(2,1)}), bf16[16,20,128]{2,1,0:T(8,128)(2,1)S(1)}, u32[]{:S(2)}, u32[]{:S(2)}) async-start(bf16[16,20,128]{2,1,0:T(8,128)(2,1)} %reshape.694), calls=%async_computation.10 | async-start | bytes 196608 | tf_op jit(solution)/shard_map/all_to_all | solution.py:101
  390.1 17.9 %all-to-all-start.13 = ((bf16[128,9,128]{2,1,0:T(8,128)(2,1)}), bf16[128,9,128]{2,1,0:T(8,128)(2,1)S(1)}, u32[]{:S(2)}, u32[]{:S(2)}) async-start(bf16[128,9,128]{2,1,0:T(8,128)(2,1)} %reshape.699), calls=%async_computation.13 | async-start | bytes 1048576 | tf_op jit(solution)/shard_map/all_to_all | solution.py:101
  463.1 43.4 %collective-permute-start.35 = (bf16[128,2048]{1,0:T(8,128)(2,1)}, bf16[128,2048]{1,0:T(8,128)(2,1)S(1)}, u32[]{:S(2)}, u32[]{:S(2)}) collective-permute-start(bf16[128,2048]{1,0:T(8,128)(2,1)} %get-tuple-element.57), channel_id=1, source_target_pairs={{0,2},{2,4},{4,6},{6,0},{1,3},{3,5},{5,7},{7,1},{8,10},{10,12},{12... | collective-permute-start | bytes 1572872 | tf_op jit(solution)/shard_map/ppermute | solution.py:29
  463.1 43.4 %collective-permute-start.39 = (bf16[128,2048]{1,0:T(8,128)(2,1)}, bf16[128,2048]{1,0:T(8,128)(2,1)S(1)}, u32[]{:S(2)}, u32[]{:S(2)}) collective-permute-start(bf16[128,2048]{1,0:T(8,128)(2,1)} %get-tuple-element.58), channel_id=1, source_target_pairs={{0,6},{2,0},{4,2},{6,4},{1,7},{3,1},{5,3},{7,5},{8,14},{10,8},{12,... | collective-permute-start | bytes 1572872 | tf_op jit(solution)/shard_map/ppermute | solution.py:33
  478.3 52.0 %collective-permute-start.38 = (bf16[128,2048]{1,0:T(8,128)(2,1)}, bf16[128,2048]{1,0:T(8,128)(2,1)S(1)}, u32[]{:S(2)}, u32[]{:S(2)}) collective-permute-start(bf16[128,2048]{1,0:T(8,128)(2,1)} %get-tuple-element.59), channel_id=1, source_target_pairs={{0,2},{2,4},{4,6},{6,0},{1,3},{3,5},{5,7},{7,1},{8,10},{10,12},{12... | collective-permute-start | bytes 1572872 | tf_op jit(solution)/shard_map/ppermute | solution.py:29
  478.3 61.0 %collective-permute-start.37 = (bf16[128,2048]{1,0:T(8,128)(2,1)}, bf16[128,2048]{1,0:T(8,128)(2,1)S(1)}, u32[]{:S(2)}, u32[]{:S(2)}) collective-permute-start(bf16[128,2048]{1,0:T(8,128)(2,1)} %get-tuple-element.60), channel_id=1, source_target_pairs={{0,6},{2,0},{4,2},{6,4},{1,7},{3,1},{5,3},{7,5},{8,14},{10,8},{12,... | collective-permute-start | bytes 1572872 | tf_op jit(solution)/shard_map/ppermute | solution.py:33
  481.6 17.8 %all-to-all-start.4 = ((bf16[128,6,128]{2,1,0:T(8,128)(2,1)}), bf16[128,6,128]{2,1,0:T(8,128)(2,1)S(1)}, u32[]{:S(2)}, u32[]{:S(2)}) async-start(bf16[128,6,128]{2,1,0:T(8,128)(2,1)} %reshape.684), calls=%async_computation.4 | async-start | bytes 524288 | tf_op jit(solution)/shard_map/all_to_all | solution.py:101
  500.3 20.1 %all-to-all-start.14 = ((bf16[128,9,128]{2,1,0:T(8,128)(2,1)}), bf16[128,9,128]{2,1,0:T(8,128)(2,1)S(1)}, u32[]{:S(2)}, u32[]{:S(2)}) async-start(bf16[128,9,128]{2,1,0:T(8,128)(2,1)} %broadcast_in_dim.63), calls=%async_computation.14 | async-start | bytes 1048576 | tf_op jit(solution)/shard_map/all_to_all | solution.py:101
  509.2 21.1 %collective-permute-start.40 = (bf16[128,2048]{1,0:T(8,128)(2,1)}, bf16[128,2048]{1,0:T(8,128)(2,1)}, u32[]{:S(2)}, u32[]{:S(2)}) collective-permute-start(bf16[128,2048]{1,0:T(8,128)(2,1)} %get-tuple-element.56), channel_id=1, source_target_pairs={{0,6},{2,0},{4,2},{6,4},{1,7},{3,1},{5,3},{7,5},{8,14},{10,8},{12,... | collective-permute-start | bytes 1572872 | tf_op jit(solution)/shard_map/ppermute | solution.py:33
  (210 other events, 2189.3 us)
